TPU v7x, 32 devices: a whole 2x2x4 slice. The times are simulated.
32 devices in a mesh: expert: 8 (over z, x), tensor: 4 (over y, core).
Axes of the slice: x: 2, y: 2, z: 4, core: 2. Of those that a mesh axis runs over, the one named last changes fastest.
Arguments:
- tokens: bfloat16 [4096, 768], P('expert'), may hold values from -6 to 6
- doc_lengths: int32 [8, 4], P('expert'), may hold values from 1 to 256, 512 in all within a row
- routes: int32 [4096, 1], P('expert'), may hold values from 0 to 7; in each aligned block of 512 rows (0 to 511, 512 to 1023, ...) at most 128 rows name the same one
- gain_first: float32 [768], replicated, may hold values from 0.5 to 1.5
- projections: bfloat16 [3, 768, 768], P(None, None, 'tensor'), may hold values from -0.21875 to 0.21875
- attention_out: bfloat16 [768, 768], P('tensor'), may hold values from -1.75 to 1.75
- relative_bias_table: float32 [32, 12], P(None, 'tensor'), may hold values from -4 to 4
- gain_second: float32 [768], replicated, may hold values from 0.5 to 1.5
- router_weight: bfloat16 [768, 8], replicated, may hold values from -0.15625 to 0.15625
- expert_in: bfloat16 [8, 768, 3072], P('expert', None, 'tensor'), may hold values from -0.21875 to 0.21875
- expert_out: bfloat16 [8, 3072, 768], P('expert', 'tensor'), may hold values from -2 to 2
- cotangent: bfloat16 [4096, 768], P('expert'), may hold values from -6 to 6
Outputs:
- layer_output: bfloat16 [4096, 768], P('expert')
- grad_tokens: float32 [4096, 768], P('expert')
- grad_gain_first: float32 [768], replicated
- grad_projections: float32 [3, 768, 768], P(None, None, 'tensor')
- grad_attention_out: float32 [768, 768], P('tensor')
- grad_position_table: float32 [32, 12], P(None, 'tensor')
- grad_gain_second: float32 [768], replicated
- grad_router: float32 [768, 8], replicated
- grad_expert_in: float32 [8, 768, 3072], P('expert', None, 'tensor')
- grad_expert_out: float32 [8, 3072, 768], P('expert', 'tensor')
Inputs may be any that keep to these rules, and one draw needn't show every extreme that they name: `doc_lengths`: each row sums to 512; its longest entry is exactly 256. `routes`: among the 512 rows of one token group no expert is named more than 128 times; in some group one expert is named exactly 128 times; every expert is named somewhere.
All inputs are finite; a program needn't handle non-finite values.
Results may differ from a plain program's by a relative error of at most 0.013.
The roundings to bfloat16 on the way count: a program that leaves them out, or rounds other values in their place, can miss the bound.
Values may be sent and summed in bfloat16 or wider, within the bound.
A program may use at most 128 MiB of HBM per device.

v0:
```python
import math

import jax
import jax.numpy as jnp
from jax import lax
from jax.sharding import PartitionSpec as P

edge_list = (1, 2, 3, 4, 5, 6, 7, 8, 12, 16, 23, 32, 46, 64, 91)
tiny_eps = 1e-06
masked_score = -1e30
largest_logit = lax.Precision.HIGHEST


def bucket_table(row_count):
    places = jnp.arange(row_count, dtype=jnp.int32)
    offsets = places[:, None] - places[None, :]
    distance = jnp.abs(offsets)
    bounds = jnp.asarray(edge_list, dtype=jnp.int32)
    passed = jnp.sum((distance[:, :, None] >= bounds[None, None, :]).astype(jnp.int32), axis=2)
    return passed + 16 * (offsets < 0).astype(jnp.int32)


def document_mask(lengths_row, row_count):
    places = jnp.arange(row_count, dtype=jnp.int32)
    endings = jnp.cumsum(lengths_row)
    document = jnp.sum((places[:, None] >= endings[None, :]).astype(jnp.int32), axis=1)
    return document[:, None] == document[None, :]


def rms_scale(values, gain):
    return values * lax.rsqrt(jnp.mean(values * values, axis=-1, keepdims=True) + tiny_eps) * gain


def gelu_curve(values):
    return (
        0.5
        * values
        * (1.0 + jnp.tanh(0.7978845608 * (values + 0.044715 * values * values * values)))
    )


def softmax_rows(scores):
    top_score = jnp.max(scores, axis=-1, keepdims=True)
    raised = jnp.exp(scores - top_score)
    return raised / jnp.sum(raised, axis=-1, keepdims=True)


def tensor_total(value):
    return lax.psum(value, "tensor")


def to_experts(buffer):
    return lax.all_to_all(buffer, "expert", split_axis=0, concat_axis=0, tiled=True)


def from_experts(partial_rows):
    summed = lax.psum(partial_rows, "tensor").astype(jnp.bfloat16)
    return lax.all_to_all(summed, "expert", split_axis=0, concat_axis=0, tiled=True)


def into_rows(received, local_count):
    sources = received.shape[0]
    model_width = received.shape[2]
    capacity = received.shape[1] // local_count
    arranged = received.reshape(sources, local_count, capacity, model_width).transpose(1, 0, 2, 3)
    return arranged.reshape(local_count, sources * capacity, model_width)


def out_of_rows(rows, sources):
    local_count = rows.shape[0]
    model_width = rows.shape[2]
    capacity = rows.shape[1] // sources
    arranged = rows.reshape(local_count, sources, capacity, model_width).transpose(1, 0, 2, 3)
    return arranged.reshape(sources, local_count * capacity, model_width)


def bias_from_table(relative_bias_table, bucket_ids):
    buckets_total = relative_bias_table.shape[0]
    row_count = bucket_ids.shape[0]
    block = math.gcd(row_count, 128)
    labels = jnp.arange(buckets_total, dtype=jnp.int32)

    def one_block(ids):
        expert_indicator = (labels[:, None, None] == ids[None]).astype(jnp.float32)
        return jnp.einsum(
            "ft,fwx->twx", relative_bias_table, expert_indicator, precision=largest_logit
        )

    blocks = lax.map(one_block, bucket_ids.reshape(row_count // block, block, row_count))
    return jnp.transpose(blocks, (1, 0, 2, 3)).reshape(
        relative_bias_table.shape[1], row_count, row_count
    )


def scores_for(queries, keys_here, position_bias, allowed, score_scale):
    raw_scores = (
        jnp.einsum("qhd,khd->hqk", queries, keys_here, preferred_element_type=jnp.float32)
        * score_scale
        + position_bias
    )
    return jnp.where(allowed[None], raw_scores, masked_score)


def bucket_sums(grad_scores, bucket_ids, buckets_total):
    heads_here = grad_scores.shape[0]
    row_count = grad_scores.shape[1]
    block = math.gcd(row_count, 128)
    labels = jnp.arange(buckets_total, dtype=jnp.int32)

    def accumulate_block(carry, start):
        ids = lax.dynamic_slice_in_dim(bucket_ids, start, block, 0)
        expert_indicator = (
            (labels[:, None, None] == ids[None])
            .astype(jnp.bfloat16)
            .reshape(buckets_total, block * row_count)
        )
        part = lax.dynamic_slice_in_dim(grad_scores, start, block, 1).reshape(
            heads_here, block * row_count
        )
        return (
            carry
            + jnp.einsum("hx,bx->bh", part, expert_indicator, preferred_element_type=jnp.float32),
            None,
        )

    starts = jnp.arange(row_count // block, dtype=jnp.int32) * block
    total, unused = lax.scan(
        accumulate_block, jnp.zeros((buckets_total, heads_here), jnp.float32), starts
    )
    return total


def on_device(
    tokens,
    doc_lengths,
    routes,
    gain_first,
    projections,
    attention_out,
    relative_bias_table,
    gain_second,
    router_weight,
    expert_in,
    expert_out,
    cotangent,
):
    row_count = tokens.shape[0]
    model_width = tokens.shape[1]
    heads_here = relative_bias_table.shape[1]
    buckets_total = relative_bias_table.shape[0]
    head_size = projections.shape[2] // heads_here
    experts_total = router_weight.shape[1]
    local_experts = expert_in.shape[0]
    sources = lax.axis_size("expert")
    capacity = max(2, 2 * row_count // experts_total)
    score_scale = head_size ** (-0.5)
    allowed = document_mask(doc_lengths[0], row_count)
    bucket_ids = bucket_table(row_count)
    token_float = tokens.astype(jnp.float32)
    normed_float, first_back = jax.vjp(rms_scale, token_float, gain_first)
    normed_first = normed_float.astype(jnp.bfloat16)
    projected = jnp.einsum(
        "nd,cdh->cnh", normed_first, projections, preferred_element_type=jnp.float32
    ).astype(jnp.bfloat16)
    queries = projected[0].reshape(row_count, heads_here, head_size)
    keys_here = projected[1].reshape(row_count, heads_here, head_size)
    values_here = projected[2].reshape(row_count, heads_here, head_size)
    position_bias = bias_from_table(relative_bias_table, bucket_ids)
    scores = scores_for(queries, keys_here, position_bias, allowed, score_scale)
    top_score = jnp.max(scores, axis=-1, keepdims=True)
    raised = jnp.exp(scores - top_score)
    totals = jnp.sum(raised, axis=-1, keepdims=True)
    soft_weights = raised / totals
    log_total = top_score + jnp.log(totals)
    mixed_heads = jnp.einsum(
        "hqk,khd->qhd",
        soft_weights.astype(jnp.bfloat16),
        values_here,
        preferred_element_type=jnp.float32,
    )
    mixed_heads = mixed_heads.reshape(row_count, heads_here * head_size).astype(jnp.bfloat16)
    after_attention = token_float + tensor_total(
        jnp.dot(mixed_heads, attention_out, preferred_element_type=jnp.float32)
    )
    second_float, second_back = jax.vjp(rms_scale, after_attention, gain_second)
    normed_second = second_float.astype(jnp.bfloat16)
    normed_wide = normed_second.astype(jnp.float32)
    router_float = router_weight.astype(jnp.float32)
    router_probs = softmax_rows(jnp.dot(normed_wide, router_float, precision=largest_logit))
    route_column = routes[:, 0]
    chosen = route_column[:, None] == jnp.arange(experts_total, dtype=jnp.int32)[None, :]
    earlier = jnp.cumsum(chosen.astype(jnp.int32), axis=0) - 1
    capacity_position = jnp.sum(jnp.where(chosen, earlier, 0), axis=1)
    row_index = route_column * capacity + capacity_position
    gate_value = jnp.sum(jnp.where(chosen, router_probs, 0.0), axis=1)
    send_rows = (
        jnp.zeros((experts_total * capacity, model_width), jnp.bfloat16)
        .at[row_index]
        .set(normed_second)
    )
    expert_rows = into_rows(
        to_experts(send_rows.reshape(sources, local_experts * capacity, model_width)), local_experts
    )
    pre_active = jnp.einsum(
        "erd,edf->erf", expert_rows, expert_in, preferred_element_type=jnp.float32
    )
    hidden_float, gelu_back = jax.vjp(gelu_curve, pre_active)
    hidden_units = hidden_float.astype(jnp.bfloat16)
    partial_rows = jnp.einsum(
        "erf,efd->erd", hidden_units, expert_out, preferred_element_type=jnp.float32
    )
    returned = from_experts(out_of_rows(partial_rows, sources)).reshape(
        experts_total * capacity, model_width
    )
    picked = returned[row_index].astype(jnp.float32)
    layer_output = (after_attention + gate_value[:, None] * picked).astype(jnp.bfloat16)
    upstream = cotangent.astype(jnp.float32)
    grad_gate = jnp.sum(upstream * picked, axis=1)
    grad_outgoing = (gate_value[:, None] * upstream).astype(jnp.bfloat16)
    grad_buffer_rows = (
        jnp.zeros((experts_total * capacity, model_width), jnp.bfloat16)
        .at[row_index]
        .set(grad_outgoing)
    )
    grad_rows = into_rows(
        to_experts(grad_buffer_rows.reshape(sources, local_experts * capacity, model_width)),
        local_experts,
    )
    grad_hidden = jnp.einsum(
        "erd,efd->erf", grad_rows, expert_out, preferred_element_type=jnp.float32
    )
    grad_expert_out = jnp.einsum(
        "erf,erd->efd", hidden_units, grad_rows, preferred_element_type=jnp.float32
    )
    grad_pre = gelu_back(grad_hidden)[0].astype(jnp.bfloat16)
    grad_expert_in = jnp.einsum(
        "erd,erf->edf", expert_rows, grad_pre, preferred_element_type=jnp.float32
    )
    grad_inputs = jnp.einsum(
        "erf,edf->erd", grad_pre, expert_in, preferred_element_type=jnp.float32
    )
    back_rows = from_experts(out_of_rows(grad_inputs, sources)).reshape(
        experts_total * capacity, model_width
    )
    grad_from_experts = back_rows[row_index].astype(jnp.float32)
    grad_logits = router_probs * (
        jnp.where(chosen, grad_gate[:, None], 0.0) - (gate_value * grad_gate)[:, None]
    )
    grad_router = jnp.dot(normed_wide.T, grad_logits, precision=largest_logit)
    grad_normed_second = grad_from_experts + jnp.dot(
        grad_logits, router_float.T, precision=largest_logit
    )
    grad_after, grad_gain_second = second_back(grad_normed_second)
    grad_residual = upstream + grad_after
    grad_attention_low = grad_residual.astype(jnp.bfloat16)
    grad_attention_out = jnp.einsum(
        "nh,nd->hd", mixed_heads, grad_attention_low, preferred_element_type=jnp.float32
    )
    grad_mixed = jnp.einsum(
        "nd,hd->nh", grad_attention_low, attention_out, preferred_element_type=jnp.float32
    )
    grad_mixed = grad_mixed.astype(jnp.bfloat16).reshape(row_count, heads_here, head_size)
    recomputed_scores = scores_for(queries, keys_here, position_bias, allowed, score_scale)
    soft_again = jnp.exp(recomputed_scores - log_total)
    grad_soft = jnp.einsum(
        "qhd,khd->hqk", grad_mixed, values_here, preferred_element_type=jnp.float32
    )
    grad_values = jnp.einsum(
        "hqk,qhd->khd",
        soft_again.astype(jnp.bfloat16),
        grad_mixed,
        preferred_element_type=jnp.float32,
    ).astype(jnp.bfloat16)
    grad_scores = (
        soft_again * (grad_soft - jnp.sum(soft_again * grad_soft, axis=-1, keepdims=True))
    ).astype(jnp.bfloat16)
    grad_position_table = bucket_sums(grad_scores, bucket_ids, buckets_total)
    grad_queries = (
        jnp.einsum("hqk,khd->qhd", grad_scores, keys_here, preferred_element_type=jnp.float32)
        * score_scale
    ).astype(jnp.bfloat16)
    grad_keys = (
        jnp.einsum("hqk,qhd->khd", grad_scores, queries, preferred_element_type=jnp.float32)
        * score_scale
    ).astype(jnp.bfloat16)
    grad_projected = jnp.stack([grad_queries, grad_keys, grad_values]).reshape(
        3, row_count, heads_here * head_size
    )
    grad_projections = jnp.einsum(
        "nd,cnh->cdh", normed_first, grad_projected, preferred_element_type=jnp.float32
    )
    grad_normed_first = tensor_total(
        jnp.einsum("cnh,cdh->nd", grad_projected, projections, preferred_element_type=jnp.float32)
    )
    grad_first_in, grad_gain_first = first_back(grad_normed_first)
    grad_tokens = grad_residual + grad_first_in
    summed = lax.psum(
        (
            grad_projections,
            grad_attention_out,
            grad_position_table,
            grad_gain_first,
            grad_gain_second,
            grad_router,
        ),
        "expert",
    )
    return (
        layer_output,
        grad_tokens,
        summed[3],
        summed[0],
        summed[1],
        summed[2],
        summed[4],
        summed[5],
        grad_expert_in,
        grad_expert_out,
    )


def solution(mesh):
    placed = (
        P("expert", None),
        P("expert", None),
        P("expert", None),
        P(),
        P(None, None, "tensor"),
        P("tensor", None),
        P(None, "tensor"),
        P(),
        P(),
        P("expert", None, "tensor"),
        P("expert", "tensor", None),
        P("expert", None),
    )
    return jax.shard_map(
        on_device,
        mesh=mesh,
        in_specs=placed,
        out_specs=(
            P("expert", None),
            P("expert", None),
            P(),
            P(None, None, "tensor"),
            P("tensor", None),
            P(None, "tensor"),
            P(),
            P(),
            P("expert", None, "tensor"),
            P("expert", "tensor", None),
        ),
        check_vma=False,
    )
```

profile of v0, /device:TPU:0, one launch (start us, length us, event | category | flops | bytes accessed | tf_op | source)
XLA Modules:
  0.0 565.7 jit_solution(13777713198093759473)
XLA Ops:
  15.3 14.5 %while.22 = (s32[]{:T(128)}, f32[4,3,128,512]{3,1,2,0:T(4,128)}, s32[4,128,512]{2,1,0:T(8,128)S(1)}, f32[32,3]{0,1:T(4,128)S(1)}, s32[]{:T(128)}) while((s32[]{:T(128)}, f32[4,3,128,512]{3,1,2,0:T(4,128)}, s32[4,128,512]{2,1,0:T(8,128)S(1)}, f32[32,3]{0,1:T(4,128)S(1)}, s32[]{:T(128)}) %tuple.71), condition=%wide.region_5.6_spmd.clone, body=%wide.region_4.5_spmd.clone.sunk | while | flops 77594624 | bytes 1835469 | solution.py:89
  15.4 3.6 fusion.126
  29.8 4.9 copy.45
  43.6 44.1 %all-reduce.8.cloned.1.call-done = f32[512,768]{1,0:T(8,128)} async-done(((f32[512,768]{1,0:T(8,128)}), f32[512,768]{1,0:T(8,128)}) %all-reduce.8.cloned.1.call-update) | async-done | bytes 1572880 | tf_op jit(solution)/shard_map/psum | solution.py:49
  90.1 3.9 scatter_custom_fusion
  93.9 5.7 %all-to-all-start = ((bf16[8,128,768]{2,1,0:T(8,128)(2,1)}), bf16[8,128,768]{2,1,0:T(8,128)(2,1)}, u32[]{:S(2)}, u32[]{:S(2)}) async-start(bf16[8,128,768]{2,1,0:T(8,128)(2,1)} %bitcast.135), calls=%async_computation | async-start | bytes 3145728 | tf_op jit(solution)/shard_map/all_to_all | solution.py:53
  102.9 4.5 scatter_custom_fusion.1
  107.4 29.2 %all-to-all-done = bf16[8,128,768]{2,1,0:T(8,128)(2,1)} async-done(((bf16[8,128,768]{2,1,0:T(8,128)(2,1)}), bf16[8,128,768]{2,1,0:T(8,128)(2,1)}, u32[]{:S(2)}, u32[]{:S(2)}) %all-to-all-start) | async-done | bytes 1572896 | tf_op jit(solution)/shard_map/all_to_all | solution.py:53
  136.6 4.3 all-to-all-start.2
  140.9 4.9 multiply_convert_fusion.1
  150.0 27.5 %all-to-all-done.2 = bf16[8,128,768]{2,1,0:T(8,128)(2,1)} async-done(((bf16[8,128,768]{2,1,0:T(8,128)(2,1)}), bf16[8,128,768]{2,1,0:T(8,128)(2,1)}, u32[]{:S(2)}, u32[]{:S(2)}) %all-to-all-start.2) | async-done | bytes 1572896 | tf_op jit(solution)/shard_map/all_to_all | solution.py:53
  177.5 6.1 %fusion.16 = bf16[1024,768]{1,0:T(8,128)(2,1)S(1)} fusion(f32[1024,768]{1,0:T(8,128)} %get-tuple-element.156, bf16[1024,768]{1,0:T(8,128)(2,1)} %bitcast.28, bf16[1,768,768]{2,1,0:T(8,128)(2,1)} %param.27), kind=kOutput, calls=%fused_computation.28 | convolution fusion | flops 1226833920 | bytes 7471104 | tf_op jit(solution)/shard_map/erd,efd->erf/dot_general | solution.py:229
  187.9 111.1 %all-reduce.13 = (bf16[8,128,768]{2,1,0:T(8,128)(2,1)}, bf16[8,128,768]{2,1,0:T(8,128)(2,1)}) all-reduce(f32[8,128,768]{2,1,0:T(8,128)} %fusion.38, f32[8,128,768]{2,1,0:T(8,128)} %fusion.36), channel_id=1, replica_groups=mesh['expert'=8,'tensor'=4] {'tensor'}, use_global_device_ids=true, to_apply=%region_17.18 | all-reduce | flops 1572864 | bytes 9437184 | tf_op jit(solution)/shard_map/psum | solution.py:57
  299.0 42.4 %all_to_all.20 = bf16[8,128,768]{2,1,0:T(8,128)(2,1)} all-to-all(bf16[8,128,768]{2,1,0:T(8,128)(2,1)} %get-tuple-element.144), channel_id=1, replica_groups=mesh['expert'=8,'tensor'=4] {'expert'}, dimensions={0} | all-to-all | bytes 3145728 | tf_op jit(solution)/shard_map/all_to_all | solution.py:58
  341.4 4.4 all-to-all-start.3
  348.5 4.4 convolution_bitcast_fusion
  352.8 4.3 convolution_bitcast_fusion.1
  357.1 4.8 gather_fusion
  363.3 19.4 %all-to-all-done.3 = bf16[8,128,768]{2,1,0:T(8,128)(2,1)} async-done(((bf16[8,128,768]{2,1,0:T(8,128)(2,1)}), bf16[8,128,768]{2,1,0:T(8,128)(2,1)}, u32[]{:S(2)}, u32[]{:S(2)}) %all-to-all-start.3) | async-done | bytes 1572896 | tf_op jit(solution)/shard_map/all_to_all | solution.py:58
  382.8 4.7 gather_fusion.1
  407.9 22.3 %while.23 = (s32[]{:T(128)}, f32[32,3]{0,1:T(4,128)S(1)}, s32[4]{0:T(128)S(1)}, s32[512,512]{1,0:T(8,128)}, bf16[3,512,512]{1,2,0:T(8,128)(2,1)S(1)}, /*index=5*/s32[]{:T(128)}, s32[]{:T(128)}, s32[]{:T(128)}) while((s32[]{:T(128)}, f32[32,3]{0,1:T(4,128)S(1)}, s32[4]{0:T(128)S(1)}, s32[512,512]{1,0:T(8,128)}, ...), condition=%wide.region_30.31_spmd.clone, body=%wide.region_29.30_spmd.clone.sunk | while | flops 14680262 | bytes 2753437 | solution.py:127
  430.2 10.5 %all-reduce.10.cloned.1.call-done = f32[512,768]{1,0:T(8,128)} async-done(((f32[512,768]{1,0:T(8,128)}), f32[512,768]{1,0:T(8,128)}) %all-reduce.10.cloned.1.call-update) | async-done | bytes 1572880 | tf_op jit(solution)/shard_map/psum | solution.py:49
  442.7 40.1 %all-reduce = (f32[768]{0:T(1024)}, f32[32,3]{0,1:T(4,128)}, f32[768]{0:T(1024)}, f32[768,8]{0,1:T(8,128)}) all-reduce(f32[768]{0:T(1024)S(1)} %get-tuple-element.118, f32[32,3]{0,1:T(4,128)S(1)} %get-tuple-element.70, f32[768]{0:T(1024)S(1)} %copy-done.58, ...), channel_id=1, replica_groups=mesh['expert'=8,'tensor'=4] {'expert'}, use_global_device_ids=true, to_apply=%region_26.27 | all-reduce | flops 7776 | bytes 62208 | tf_op jit(solution)/shard_map/psum | solution.py:297
  485.8 69.2 %all-reduce.12.cloned.1.call-done = (f32[3,768,192]{1,2,0:T(8,128)}, f32[192,768]{1,0:T(8,128)}) async-done(((f32[3,768,192]{1,2,0:T(8,128)}, f32[192,768]{1,0:T(8,128)}), (f32[3,768,192]{1,2,0:T(8,128)}, f32[192,768]{1,0:T(8,128)})) %all-reduce.12.cloned.1.call-update) | async-done | bytes 2359312 | tf_op jit(solution)/shard_map/psum | solution.py:297
  (238 shorter events, 88.9 us)
Async XLA Ops:
  7.2 133.7 %copy-start = (bf16[1,768,768]{2,1,0:T(8,128)(2,1)S(1)}, bf16[1,768,768]{2,1,0:T(8,128)(2,1)}, u32[]{:S(2)}) copy-start(bf16[1,768,768]{2,1,0:T(8,128)(2,1)} %param.26) | copy-start | bytes 3538948
  7.2 80.5 %all-reduce.8.cloned.1.call-start = ((), (), s32[]{:S(2)}) async-start(), calls=%async_computation.4 | async-start | bytes 3145728 | tf_op jit(solution)/shard_map/psum | solution.py:49
  12.4 22.3 %copy-start.13 = (bf16[1,512,192]{1,2,0:T(8,128)(2,1)}, bf16[1,512,192]{1,2,0:T(8,128)(2,1)S(1)}, u32[]{:S(2)}) copy-start(bf16[1,512,192]{1,2,0:T(8,128)(2,1)S(1)} %get-tuple-element.150) | copy-start | bytes 589828
  12.4 22.3 %copy-start.15 = (bf16[1,512,192]{1,2,0:T(8,128)(2,1)}, bf16[1,512,192]{1,2,0:T(8,128)(2,1)S(1)}, u32[]{:S(2)}) copy-start(bf16[1,512,192]{1,2,0:T(8,128)(2,1)S(1)} %get-tuple-element.151) | copy-start | bytes 589828
  43.6 46.4 %copy-start.62 = (s32[512,1]{0,1:T(1,128)}, s32[512,1]{0,1:T(1,128)S(1)}, u32[]{:S(2)}) copy-start(s32[512,1]{0,1:T(1,128)S(1)} %compare_select_fusion) | copy-start | bytes 6148
  43.6 46.4 %copy-start.36 = (f32[768]{0:T(1024)S(1)}, f32[768]{0:T(1024)}, u32[]{:S(2)}) copy-start(f32[768]{0:T(1024)} %param.24) | copy-start | bytes 9220
  90.0 9.6 %copy-start.40 = (f32[512]{0:T(512)}, f32[512]{0:T(512)S(1)}, u32[]{:S(2)}) copy-start(f32[512]{0:T(512)S(1)} %fusion.81) | copy-start | bytes 6148
  93.9 42.6 %all-to-all-start = ((bf16[8,128,768]{2,1,0:T(8,128)(2,1)}), bf16[8,128,768]{2,1,0:T(8,128)(2,1)}, u32[]{:S(2)}, u32[]{:S(2)}) async-start(bf16[8,128,768]{2,1,0:T(8,128)(2,1)} %bitcast.135), calls=%async_computation | async-start | bytes 3145728 | tf_op jit(solution)/shard_map/all_to_all | solution.py:53
  136.6 40.9 %all-to-all-start.2 = ((bf16[8,128,768]{2,1,0:T(8,128)(2,1)}), bf16[8,128,768]{2,1,0:T(8,128)(2,1)}, u32[]{:S(2)}, u32[]{:S(2)}) async-start(bf16[8,128,768]{2,1,0:T(8,128)(2,1)} %bitcast.134), calls=%async_computation.2 | async-start | bytes 3145728 | tf_op jit(solution)/shard_map/all_to_all | solution.py:53
  140.9 6.1 %copy-start.66 = (bf16[1,768,768]{2,1,0:T(8,128)(2,1)S(1)}, bf16[1,768,768]{2,1,0:T(8,128)(2,1)}, u32[]{:S(2)}) copy-start(bf16[1,768,768]{2,1,0:T(8,128)(2,1)} %param.27) | copy-start | bytes 3538948
  341.4 5.3 copy-start.35
  341.4 5.3 copy-start.48
  341.4 6.0 %copy-start.8 = (s32[512,512]{1,0:T(8,128)S(1)}, s32[512,512]{1,0:T(8,128)}, u32[]{:S(2)}) copy-start(s32[512,512]{1,0:T(8,128)} %copy-done.7) | copy-start | bytes 3145732
  341.4 41.3 %all-to-all-start.3 = ((bf16[8,128,768]{2,1,0:T(8,128)(2,1)}), bf16[8,128,768]{2,1,0:T(8,128)(2,1)}, u32[]{:S(2)}, u32[]{:S(2)}) async-start(bf16[8,128,768]{2,1,0:T(8,128)(2,1)} %get-tuple-element.145), calls=%async_computation.3 | async-start | bytes 3145728 | tf_op jit(solution)/shard_map/all_to_all | solution.py:58
  345.8 94.9 %all-reduce.10.cloned.1.call-start = ((), (), s32[]{:S(2)}) async-start(), calls=%async_computation.5 | async-start | bytes 3145728 | tf_op jit(solution)/shard_map/psum | solution.py:49
  363.3 24.2 %copy-start.44 = (f32[512]{0:T(512)}, f32[512]{0:T(512)S(1)}, u32[]{:S(2)}) copy-start(f32[512]{0:T(512)S(1)} %fusion.28) | copy-start | bytes 6148
  363.3 24.2 %copy-start.50 = (f32[512]{0:T(512)}, f32[512]{0:T(512)S(1)}, u32[]{:S(2)}) copy-start(f32[512]{0:T(512)S(1)} %mul.275) | copy-start | bytes 6148
  399.6 155.4 %all-reduce.12.cloned.1.call-start = ((), (), s32[]{:S(2)}) async-start(), calls=%async_computation.6 | async-start | bytes 4718592 | tf_op jit(solution)/shard_map/psum | solution.py:297
  407.8 32.9 %copy-start.55 = (f32[512]{0:T(512)S(1)}, f32[512]{0:T(512)}, u32[]{:S(2)}) copy-start(f32[512]{0:T(512)} %copy-done.53) | copy-start | bytes 6148
  407.8 32.9 %copy-start.61 = (f32[768]{0:T(1024)S(1)}, f32[768]{0:T(1024)}, u32[]{:S(2)}) copy-start(f32[768]{0:T(1024)} %param.20) | copy-start | bytes 9220
  430.1 12.6 %copy-start.30 = (f32[768,8]{0,1:T(8,128)S(1)}, f32[768,8]{0,1:T(8,128)}, u32[]{:S(2)}) copy-start(f32[768,8]{0,1:T(8,128)} %fusion.71) | copy-start | bytes 73732
  430.1 12.6 %copy-start.58 = (f32[768]{0:T(1024)S(1)}, f32[768]{0:T(1024)}, u32[]{:S(2)}) copy-start(f32[768]{0:T(1024)} %get-tuple-element.116) | copy-start | bytes 9220
  430.1 52.7 %copy-start.57 = (f32[512]{0:T(512)S(1)}, f32[512]{0:T(512)}, u32[]{:S(2)}) copy-start(f32[512]{0:T(512)} %copy-done.56) | copy-start | bytes 6148
  430.2 52.7 %copy-start.5 = (f32[512,768]{1,0:T(8,128)S(1)}, f32[512,768]{1,0:T(8,128)}, u32[]{:S(2)}) copy-start(f32[512,768]{1,0:T(8,128)} %copy-done.4) | copy-start | bytes 4718596
  (56 other events, 131.6 us)
Sparse Core Ops, SparseCore 0:
  42.2 45.5 all-reduce.7
  399.7 40.9 all-reduce.9
  444.9 110.0 all-reduce.11
where the time goes:
time: 575 us; the launch traced here: 566 us
  waiting for transfers between devices  200 us (35%)
  blocking collectives  194 us (34%)
  matrix products  67.3 us (12%)
  local copies, waits for them, and re-layouts  39 us (7%)
  other arithmetic  27.9 us (5%)
  starting transfers between devices  15 us (3%)
  between operations  14.9 us (3%)
  loops' own time  7.91 us (1%)
    psum x1, blocking collectives, from_experts(): summed = lax.psum(partial_rows, 'tensor').astype(jnp.bfloat16)  111 us
    psum x1, waiting for transfers between devices, on_device(): lax.psum((grad_projections, grad_attention_out, grad_position_table, grad...  69.2 us
    all_to_all x2, waiting for transfers between devices, to_experts(): lax.all_to_all(buffer, 'expert', split_axis=0, concat_axis=0, tiled=True)  56.7 us
    psum x2, waiting for transfers between devices, tensor_total(): return lax.psum(value, 'tensor')  54.7 us
    all_to_all x1, blocking collectives, from_experts(): lax.all_to_all(summed, 'expert', split_axis=0, concat_axis=0, tiled=True)  42.4 us
    psum x1, blocking collectives, on_device(): lax.psum((grad_projections, grad_attention_out, grad_position_table, grad...  40.1 us
    all_to_all x1, waiting for transfers between devices, from_experts(): lax.all_to_all(summed, 'expert', split_axis=0, concat_axis=0, tiled=True)  19.4 us
    unnamed x150, local copies, waits for them, and re-layouts  14.9 us
  transfers between devices with their start and end apart: 6, of which 6 were waited for; matrix products, arithmetic and copies ran while one was open for 10% of the time, Pallas kernels for 0%

commit v1 on v0

v1 whole, which is shorter than its diff:
```python
import functools

import jax
import jax.numpy as jnp
from jax import lax
from jax.experimental import pallas as pl
from jax.experimental.pallas import tpu as pltpu
from jax.sharding import PartitionSpec as P

edge_list = (1, 2, 3, 4, 5, 6, 7, 8, 12, 16, 23, 32, 46, 64, 91)
tiny_eps = 1e-06
masked_score = -1e30
largest_logit = lax.Precision.HIGHEST


def offset_buckets(row_count):
    span = 2 * row_count
    places = jnp.arange(span, dtype=jnp.int32)
    offsets = jnp.where(places < row_count, -places, span - places)
    bounds = jnp.asarray(edge_list, dtype=jnp.int32)
    passed = jnp.sum((jnp.abs(offsets)[:, None] >= bounds[None, :]).astype(jnp.int32), axis=1)
    return passed + 16 * (offsets < 0).astype(jnp.int32)


def document_ids(lengths_row, row_count):
    places = jnp.arange(row_count, dtype=jnp.int32)
    endings = jnp.cumsum(lengths_row)
    return jnp.sum((places[:, None] >= endings[None, :]).astype(jnp.int32), axis=1)


def rms_scale(values, gain):
    return values * lax.rsqrt(jnp.mean(values * values, axis=-1, keepdims=True) + tiny_eps) * gain


def gelu_curve(values):
    return (
        0.5
        * values
        * (1.0 + jnp.tanh(0.7978845608 * (values + 0.044715 * values * values * values)))
    )


def softmax_rows(scores):
    top_score = jnp.max(scores, axis=-1, keepdims=True)
    raised = jnp.exp(scores - top_score)
    return raised / jnp.sum(raised, axis=-1, keepdims=True)


MESH = pl.DeviceIdType.MESH


def vmem():
    return pl.BlockSpec(memory_space=pltpu.VMEM)


def tensor_places():
    mine = lax.axis_index("tensor")
    core = mine % 2
    side = mine // 2
    return mine, core, side, side * 2 + (1 - core), (1 - side) * 2 + core


def greet(devices):
    barrier = pltpu.get_barrier_semaphore()
    for device in devices:
        pl.semaphore_signal(barrier, inc=1, device_id=device, device_id_type=MESH)
    pl.semaphore_wait(barrier, len(devices))


def remote(source, target, send_sem, recv_sem, device):
    return pltpu.make_async_remote_copy(
        src_ref=source,
        dst_ref=target,
        send_sem=send_sem,
        recv_sem=recv_sem,
        device_id=device,
        device_id_type=MESH,
    )


def tensor_sum_kernel(x_ref, o_ref, near, chip, far, send_sem, recv_sem):
    _, core, _, sibling, across = tensor_places()
    half = x_ref.shape[0] // 2
    greet([{"tensor": sibling}, {"tensor": across}])
    own = pl.ds(pl.multiple_of(core * half, half), half)
    other = pl.ds(pl.multiple_of((1 - core) * half, half), half)
    first = remote(x_ref.at[other], near, send_sem.at[0], recv_sem.at[0], {"tensor": sibling})
    first.start()
    first.wait()
    chip[...] = (x_ref[own].astype(jnp.float32) + near[...].astype(jnp.float32)).astype(chip.dtype)
    second = remote(chip, far, send_sem.at[1], recv_sem.at[1], {"tensor": across})
    second.start()
    second.wait()
    o_ref[own] = chip[...].astype(jnp.float32) + far[...].astype(jnp.float32)
    third = remote(
        o_ref.at[own], o_ref.at[own], send_sem.at[2], recv_sem.at[2], {"tensor": sibling}
    )
    third.start()
    third.wait()


def tensor_total(value, collective_id):
    rows, width = value.shape
    if lax.axis_size("tensor") != 4 or rows % 32:
        return lax.psum(value, "tensor")
    half = pltpu.VMEM((rows // 2, width), jnp.bfloat16)
    return pl.pallas_call(
        tensor_sum_kernel,
        out_shape=jax.ShapeDtypeStruct((rows, width), jnp.float32),
        in_specs=[vmem()],
        out_specs=vmem(),
        scratch_shapes=[
            half,
            half,
            half,
            pltpu.SemaphoreType.DMA((3,)),
            pltpu.SemaphoreType.DMA((3,)),
        ],
        compiler_params=pltpu.CompilerParams(
            collective_id=collective_id, has_side_effects=True, vmem_limit_bytes=32 * 2**20
        ),
        cost_estimate=pl.CostEstimate(flops=0, bytes_accessed=30_000_000, transcendentals=0),
    )(value.astype(jnp.bfloat16))


def share_over_tensor(places, pieces, sems):
    mine, _, _, sibling, across = places
    across_send, across_recv, near_send, near_recv, pass_send, pass_recv = sems

    def begin(step):
        far = remote(
            pieces(mine, step),
            pieces(mine, step),
            across_send.at[step],
            across_recv.at[step],
            {"tensor": across},
        )
        close = remote(
            pieces(mine, step),
            pieces(mine, step),
            near_send.at[step],
            near_recv.at[step],
            {"tensor": sibling},
        )
        far.start()
        close.start()
        return far, close

    def forward(step):
        onward = remote(
            pieces(across, step),
            pieces(across, step),
            pass_send.at[step],
            pass_recv.at[step],
            {"tensor": sibling},
        )
        onward.start()
        return onward

    return begin, forward


def dispatch_kernel(groups, send_ref, o_ref, out_send, out_recv, *sems):
    here = lax.axis_index("expert")
    places = tensor_places()
    mine, _, _, sibling, across = places
    peers = [lax.rem(here + step, groups) for step in range(groups)]
    greet([{"expert": peer} for peer in peers[1:]] + [{"tensor": sibling}, {"tensor": across}])
    copies = [None]
    for step in range(1, groups):
        copy = remote(
            send_ref.at[peers[step]],
            o_ref.at[mine, here],
            out_send.at[step],
            out_recv.at[step],
            {"expert": peers[step]},
        )
        copy.start()
        copies.append(copy)
    o_ref[mine, here] = send_ref[here]

    def pieces(quarter, step):
        return o_ref.at[quarter, lax.rem(here + groups - step, groups)]

    begin, forward = share_over_tensor(places, pieces, sems)
    shared = []
    for step in range(groups):
        if step:
            copies[step].wait_recv()
        shared.append(begin(step))
    onward = []
    for step in range(groups):
        shared[step][0].wait_recv()
        onward.append(forward(step))
    for step in range(groups):
        if step:
            copies[step].wait_send()
        shared[step][0].wait_send()
        shared[step][1].wait()
        onward[step].wait()


def kernels_fit(part_rows):
    return lax.axis_size("tensor") == 4 and lax.axis_size("expert") <= 8 and part_rows % 16 == 0


def dispatch(send, collective_id):
    groups, part, width = send.shape
    if collective_id is None or not kernels_fit(part):
        received = lax.all_to_all(send, "expert", split_axis=0, concat_axis=0, tiled=True)
        return lax.all_gather(received, "tensor", axis=0, tiled=False)
    sems = pltpu.SemaphoreType.DMA((groups,))
    return pl.pallas_call(
        functools.partial(dispatch_kernel, groups),
        out_shape=jax.ShapeDtypeStruct((lax.axis_size("tensor"),) + send.shape, send.dtype),
        in_specs=[vmem()],
        out_specs=vmem(),
        scratch_shapes=[sems] * 8,
        compiler_params=pltpu.CompilerParams(
            collective_id=collective_id, has_side_effects=True, vmem_limit_bytes=32 * 2**20
        ),
        cost_estimate=pl.CostEstimate(flops=0, bytes_accessed=50_000_000, transcendentals=0),
    )(send)


def combine_kernel(groups, ahead_ref, back_ref, o_ref, near, chip, far, total, *sems):
    near_send, near_recv, far_send, far_recv, out_send, out_recv = sems[:6]
    here = lax.axis_index("expert")
    places = tensor_places()
    mine, core, side, sibling, across = places
    peers = [lax.rem(here + step, groups) for step in range(groups)]
    greet([{"expert": peer} for peer in peers[1:]] + [{"tensor": sibling}, {"tensor": across}])
    inputs = (ahead_ref, back_ref)
    sides = (1 - side, side)
    gather = []
    for kind in range(2):
        for turn in range(2):
            copy = remote(
                inputs[kind].at[sides[turn] * 2 + (1 - core)],
                near.at[2 * kind + turn],
                near_send.at[2 * kind + turn],
                near_recv.at[2 * kind + turn],
                {"tensor": sibling},
            )
            copy.start()
            gather.append(copy)
    crossing = []
    for kind in range(2):
        for turn in range(2):
            gather[2 * kind + turn].wait_recv()
            chip[2 * kind + turn] = (
                inputs[kind][sides[turn] * 2 + core].astype(jnp.float32)
                + near[2 * kind + turn].astype(jnp.float32)
            ).astype(chip.dtype)
            if turn == 0:
                copy = remote(
                    chip.at[2 * kind],
                    far.at[kind],
                    far_send.at[kind],
                    far_recv.at[kind],
                    {"tensor": across},
                )
                copy.start()
                crossing.append(copy)
    outgoing = []
    for kind in range(2):
        crossing[kind].wait_recv()
        total[kind] = (
            chip[2 * kind + 1].astype(jnp.float32) + far[kind].astype(jnp.float32)
        ).astype(total.dtype)
        outgoing.append(None)
        for step in range(1, groups):
            copy = remote(
                total.at[kind, peers[step]],
                o_ref.at[kind, mine, here],
                out_send.at[kind * groups + step],
                out_recv.at[kind * groups + step],
                {"expert": peers[step]},
            )
            copy.start()
            outgoing.append(copy)
        o_ref[kind, mine, here] = total[kind, here]

    def pieces(quarter, place):
        return o_ref.at[place // groups, quarter, lax.rem(here + groups - place % groups, groups)]

    begin, forward = share_over_tensor(places, pieces, sems[6:])
    shared = []
    for place in range(2 * groups):
        if place % groups:
            outgoing[place].wait_recv()
        shared.append(begin(place))
    onward = []
    for place in range(2 * groups):
        shared[place][0].wait_recv()
        onward.append(forward(place))
    for copy in gather + crossing:
        copy.wait_send()
    for place in range(2 * groups):
        if place % groups:
            outgoing[place].wait_send()
        shared[place][0].wait_send()
        shared[place][1].wait()
        onward[place].wait()


def combine(ahead, back, collective_id):
    quarters, groups, part, width = ahead.shape
    if not kernels_fit(part):
        both = jnp.stack([ahead, back], axis=1).astype(jnp.float32)
        mine = lax.psum_scatter(both, "tensor", scatter_dimension=0, tiled=False)
        received = lax.all_to_all(
            mine.astype(jnp.bfloat16), "expert", split_axis=1, concat_axis=1, tiled=True
        )
        return lax.all_gather(received, "tensor", axis=1, tiled=False)
    piece = (groups, part, width)
    one = pltpu.SemaphoreType.DMA((2 * groups,))
    return pl.pallas_call(
        functools.partial(combine_kernel, groups),
        out_shape=jax.ShapeDtypeStruct((2,) + ahead.shape, jnp.bfloat16),
        in_specs=[vmem(), vmem()],
        out_specs=vmem(),
        scratch_shapes=[
            pltpu.VMEM((4,) + piece, jnp.bfloat16),
            pltpu.VMEM((4,) + piece, jnp.bfloat16),
            pltpu.VMEM((2,) + piece, jnp.bfloat16),
            pltpu.VMEM((2,) + piece, jnp.bfloat16),
            pltpu.SemaphoreType.DMA((4,)),
            pltpu.SemaphoreType.DMA((4,)),
            pltpu.SemaphoreType.DMA((2,)),
            pltpu.SemaphoreType.DMA((2,)),
        ]
        + [one] * 8,
        compiler_params=pltpu.CompilerParams(
            collective_id=collective_id, has_side_effects=True, vmem_limit_bytes=40 * 2**20
        ),
        cost_estimate=pl.CostEstimate(flops=0, bytes_accessed=120_000_000, transcendentals=0),
    )(ahead, back)


def rows_dot(left, right):
    return lax.dot_general(
        left, right, (((1,), (1,)), ((), ())), preferred_element_type=jnp.float32
    )


def columns_dot(left, right):
    return lax.dot_general(
        left, right, (((0,), (0,)), ((), ())), preferred_element_type=jnp.float32
    )


def masked_scores(queries, keys_here, line, doc_column, doc_row, score_scale):
    row_count = queries.shape[0]
    bias = line
    while bias.shape[0] < row_count:
        bias = jnp.concatenate([bias, pltpu.roll(bias, bias.shape[0], 1)], axis=0)
    raw = rows_dot(queries, keys_here) * score_scale + bias[:, :row_count]
    return jnp.where(doc_column == doc_row, raw, masked_score)


def attention_kernel(heads, scale, qkv_ref, line_ref, column_ref, row_ref, mixed_ref, log_ref):
    size = qkv_ref.shape[2] // heads
    for head in range(heads):
        part = slice(head * size, head * size + size)
        scores = masked_scores(
            qkv_ref[0, :, part],
            qkv_ref[1, :, part],
            line_ref[head : head + 1, :],
            column_ref[...],
            row_ref[...],
            scale,
        )
        top_score = jnp.max(scores, axis=-1, keepdims=True)
        raised = jnp.exp(scores - top_score)
        totals = jnp.sum(raised, axis=-1, keepdims=True)
        soft = (raised / totals).astype(jnp.bfloat16)
        mixed_ref[:, part] = jnp.dot(
            soft, qkv_ref[2, :, part], preferred_element_type=jnp.float32
        ).astype(mixed_ref.dtype)
        log_ref[head] = top_score + jnp.log(totals)


def attention_back_kernel(
    heads, scale, qkv_ref, line_ref, column_ref, row_ref, log_ref, up_ref, grad_ref, sums_ref
):
    size = qkv_ref.shape[2] // heads
    row_count = qkv_ref.shape[1]
    for head in range(heads):
        part = slice(head * size, head * size + size)
        queries = qkv_ref[0, :, part]
        keys_here = qkv_ref[1, :, part]
        upstream = up_ref[:, part]
        scores = masked_scores(
            queries,
            keys_here,
            line_ref[head : head + 1, :],
            column_ref[...],
            row_ref[...],
            scale,
        )
        soft = jnp.exp(scores - log_ref[head])
        grad_soft = rows_dot(upstream, qkv_ref[2, :, part])
        centre = jnp.sum(soft * grad_soft, axis=-1, keepdims=True)
        grad_scores = (soft * (grad_soft - centre)).astype(jnp.bfloat16)
        grad_ref[2, :, part] = columns_dot(soft.astype(jnp.bfloat16), upstream).astype(
            grad_ref.dtype
        )
        grad_ref[0, :, part] = (
            jnp.dot(grad_scores, keys_here, preferred_element_type=jnp.float32) * scale
        ).astype(grad_ref.dtype)
        grad_ref[1, :, part] = (columns_dot(grad_scores, queries) * scale).astype(grad_ref.dtype)
        wide = grad_scores.astype(jnp.float32)
        wide = jnp.concatenate([wide, jnp.zeros_like(wide)], axis=1)
        while wide.shape[0] > 1:
            half = wide.shape[0] // 2
            wide = wide[:half] + pltpu.roll(wide[half:], 2 * row_count - half, 1)
        sums_ref[head : head + 1, :] = wide


def local_call(kernel, outs, args):
    return pl.pallas_call(
        kernel,
        out_shape=outs,
        in_specs=[vmem()] * len(args),
        out_specs=tuple(vmem() for _ in outs),
        compiler_params=pltpu.CompilerParams(vmem_limit_bytes=40 * 2**20),
        cost_estimate=pl.CostEstimate(
            flops=1_000_000_000, bytes_accessed=30_000_000, transcendentals=1_000_000
        ),
    )(*args)


def on_device(
    tokens,
    doc_lengths,
    routes,
    gain_first,
    projections,
    attention_out,
    relative_bias_table,
    gain_second,
    router_weight,
    expert_in,
    expert_out,
    cotangent,
):
    row_count = tokens.shape[0]
    model_width = tokens.shape[1]
    heads_here = relative_bias_table.shape[1]
    buckets_total = relative_bias_table.shape[0]
    width_here = projections.shape[2]
    head_size = width_here // heads_here
    experts_total = router_weight.shape[1]
    tensor_size = lax.axis_size("tensor")
    capacity = max(2, 2 * row_count // experts_total)
    part = capacity // tensor_size
    part_rows = experts_total * part
    score_scale = head_size ** (-0.5)
    quarter = lax.axis_index("tensor")

    route_column = routes[:, 0]
    chosen = route_column[:, None] == jnp.arange(experts_total, dtype=jnp.int32)[None, :]
    earlier = jnp.cumsum(chosen.astype(jnp.int32), axis=0) - 1
    slot = jnp.sum(jnp.where(chosen, earlier, 0), axis=1)
    place = (slot // part) * part_rows + route_column * part + slot % part
    own_place = place - quarter * part_rows
    send_pick = (
        jnp.arange(part_rows, dtype=jnp.int32)[:, None] == own_place[None, :]
    ).astype(jnp.bfloat16)
    take_pick = (
        place[:, None] == jnp.arange(tensor_size * part_rows, dtype=jnp.int32)[None, :]
    ).astype(jnp.bfloat16)

    def placed_rows(rows):
        picked_rows = jnp.dot(send_pick, rows, preferred_element_type=jnp.float32)
        return picked_rows.astype(jnp.bfloat16).reshape(experts_total, part, rows.shape[1])

    upstream_rows = dispatch(placed_rows(cotangent), None)

    token_float = tokens.astype(jnp.float32)
    normed_float, first_back = jax.vjp(rms_scale, token_float, gain_first)
    normed_first = normed_float.astype(jnp.bfloat16)
    projected = jnp.einsum(
        "nd,cdh->cnh", normed_first, projections, preferred_element_type=jnp.float32
    ).astype(jnp.bfloat16)
    bucket_pick = (
        jnp.arange(buckets_total, dtype=jnp.int32)[:, None] == offset_buckets(row_count)[None, :]
    ).astype(jnp.float32)
    bias_line = jnp.einsum("bh,bm->hm", relative_bias_table, bucket_pick, precision=largest_logit)
    documents = document_ids(doc_lengths[0], row_count)
    shared_args = (projected, bias_line, documents[:, None], documents[None, :])
    mixed_heads, log_total = local_call(
        functools.partial(attention_kernel, heads_here, score_scale),
        (
            jax.ShapeDtypeStruct((row_count, width_here), jnp.bfloat16),
            jax.ShapeDtypeStruct((heads_here, row_count, 1), jnp.float32),
        ),
        shared_args,
    )
    after_attention = token_float + tensor_total(
        jnp.dot(mixed_heads, attention_out, preferred_element_type=jnp.float32), 0
    )
    second_float, second_back = jax.vjp(rms_scale, after_attention, gain_second)
    normed_second = second_float.astype(jnp.bfloat16)
    normed_wide = normed_second.astype(jnp.float32)
    router_float = router_weight.astype(jnp.float32)
    router_probs = softmax_rows(jnp.dot(normed_wide, router_float, precision=largest_logit))
    gate_value = jnp.sum(jnp.where(chosen, router_probs, 0.0), axis=1)

    gate_high = lax.reduce_precision(gate_value, 8, 7)
    gate_rest = gate_value - gate_high
    gate_middle = lax.reduce_precision(gate_rest, 8, 7)
    gate_terms = jnp.stack([gate_high, gate_middle, gate_rest - gate_middle], axis=1)
    gate_columns = jnp.pad(gate_terms.astype(jnp.bfloat16), ((0, 0), (0, 125)))
    arrived = dispatch(placed_rows(jnp.concatenate([normed_second, gate_columns], axis=1)), 1)
    arrived = arrived.reshape(tensor_size * part_rows, model_width + 128)
    expert_rows = arrived[:, :model_width]
    row_gates = jnp.sum(
        arrived[:, model_width : model_width + 3].astype(jnp.float32), axis=1, keepdims=True
    )
    grad_rows = (
        row_gates * upstream_rows.reshape(expert_rows.shape).astype(jnp.float32)
    ).astype(jnp.bfloat16)
    weight_in = expert_in[0]
    weight_out = expert_out[0]
    pre_active = jnp.dot(expert_rows, weight_in, preferred_element_type=jnp.float32)
    hidden_float, gelu_back = jax.vjp(gelu_curve, pre_active)
    hidden_units = hidden_float.astype(jnp.bfloat16)
    partial_rows = jnp.dot(hidden_units, weight_out, preferred_element_type=jnp.float32)
    grad_hidden = rows_dot(grad_rows, weight_out)
    grad_pre = gelu_back(grad_hidden)[0].astype(jnp.bfloat16)
    grad_inputs = rows_dot(grad_pre, weight_in)
    blocks = (tensor_size, experts_total, part, model_width)
    returned = combine(
        partial_rows.astype(jnp.bfloat16).reshape(blocks),
        grad_inputs.astype(jnp.bfloat16).reshape(blocks),
        2,
    ).reshape(2, tensor_size * part_rows, model_width)
    grad_expert_out = columns_dot(hidden_units, grad_rows)[None]
    grad_expert_in = columns_dot(expert_rows, grad_pre)[None]
    picked = jnp.dot(take_pick, returned[0], preferred_element_type=jnp.float32)
    grad_from_experts = jnp.dot(take_pick, returned[1], preferred_element_type=jnp.float32)
    layer_output = (after_attention + gate_value[:, None] * picked).astype(jnp.bfloat16)
    upstream = cotangent.astype(jnp.float32)
    grad_gate = jnp.sum(upstream * picked, axis=1)
    grad_logits = router_probs * (
        jnp.where(chosen, grad_gate[:, None], 0.0) - (gate_value * grad_gate)[:, None]
    )
    grad_router = jnp.dot(normed_wide.T, grad_logits, precision=largest_logit)
    grad_normed_second = grad_from_experts + jnp.dot(
        grad_logits, router_float.T, precision=largest_logit
    )
    grad_after, grad_gain_second = second_back(grad_normed_second)
    grad_residual = upstream + grad_after
    grad_attention_low = grad_residual.astype(jnp.bfloat16)
    grad_attention_out = columns_dot(mixed_heads, grad_attention_low)
    grad_mixed = rows_dot(grad_attention_low, attention_out).astype(jnp.bfloat16)
    grad_projected, offset_sums = local_call(
        functools.partial(attention_back_kernel, heads_here, score_scale),
        (
            jax.ShapeDtypeStruct((3, row_count, width_here), jnp.bfloat16),
            jax.ShapeDtypeStruct((heads_here, 2 * row_count), jnp.float32),
        ),
        shared_args + (log_total, grad_mixed),
    )
    grad_position_table = jnp.einsum(
        "hm,bm->bh", offset_sums, bucket_pick, precision=largest_logit
    )
    grad_projections = jnp.einsum(
        "nd,cnh->cdh", normed_first, grad_projected, preferred_element_type=jnp.float32
    )
    grad_normed_first = tensor_total(
        jnp.einsum("cnh,cdh->nd", grad_projected, projections, preferred_element_type=jnp.float32),
        3,
    )
    grad_first_in, grad_gain_first = first_back(grad_normed_first)
    grad_tokens = grad_residual + grad_first_in
    large = lax.psum(
        (grad_projections.astype(jnp.bfloat16), grad_attention_out.astype(jnp.bfloat16)), "expert"
    )
    small = lax.psum(
        (grad_position_table, grad_gain_first, grad_gain_second, grad_router), "expert"
    )
    return (
        layer_output,
        grad_tokens,
        small[1],
        large[0].astype(jnp.float32),
        large[1].astype(jnp.float32),
        small[0],
        small[2],
        small[3],
        grad_expert_in,
        grad_expert_out,
    )


def solution(mesh):
    placed = (
        P("expert", None),
        P("expert", None),
        P("expert", None),
        P(),
        P(None, None, "tensor"),
        P("tensor", None),
        P(None, "tensor"),
        P(),
        P(),
        P("expert", None, "tensor"),
        P("expert", "tensor", None),
        P("expert", None),
    )
    return jax.shard_map(
        on_device,
        mesh=mesh,
        in_specs=placed,
        out_specs=(
            P("expert", None),
            P("expert", None),
            P(),
            P(None, None, "tensor"),
            P("tensor", None),
            P(None, "tensor"),
            P(),
            P(),
            P("expert", None, "tensor"),
            P("expert", "tensor", None),
        ),
        check_vma=False,
    )
```

time: 575 us -> 274 us (0.48); the launches traced: 566 us -> 273 us
  waiting for transfers between devices: 200 us -> 34.4 us
  blocking collectives: 194 us -> 36.6 us
  Pallas kernels: 0 us -> 112 us
  matrix products: 67.3 us -> 35.8 us
  local copies, waits for them, and re-layouts: 39 us -> 14.2 us
  other arithmetic: 27.9 us -> 17.9 us
  loops' own time: 7.91 us -> 0 us
  starting transfers between devices: 15 us -> 7.51 us
    psum x2 -> x1, blocking collectives: 151 us -> 36.6 us  [on_device(): lax.psum((grad_position_table, grad_gain_first, grad_gain_second, grad_ro...]
    pallas_call x0 -> x6, Pallas kernels: none -> 112 us  [the longest x1 44.1 us: combine(): pl.pallas_call(functools.partial(combine_kernel, groups), out_shape=jax.S...]
    psum x3 -> x1, waiting for transfers between devices: 124 us -> 34.3 us  [on_device(): lax.psum((grad_projections.astype(jnp.bfloat16), grad_attention_out.astyp...]
    all_to_all x3 -> x1, waiting for transfers between devices: 76.1 us -> 0.01 us  [dispatch(): lax.all_to_all(send, 'expert', split_axis=0, concat_axis=0, tiled=True)]
    all_to_all x1 -> x0, blocking collectives: 42.4 us -> none  [from_experts(): lax.all_to_all(summed, 'expert', split_axis=0, concat_axis=0, tiled=True)]
    dot_general x22 -> x14, matrix products: 54.8 us -> 27.9 us  [the longest x3 7.37 us: columns_dot(): lax.dot_general(left, right, (((0,), (0,)), ((), ())), preferred_element_...]
    gather x2 -> x0, local copies, waits for them, and re-layouts: 9.48 us -> none  [the longest x1 4.76 us: on_device(): picked = returned[row_index].astype(jnp.float32)]
    dynamic_slice x16 -> x0, local copies, waits for them, and re-layouts: 8.66 us -> none  [the longest x4 3.96 us: accumulate_block(): ids = lax.dynamic_slice_in_dim(bucket_ids, start, block, 0)]
  transfers between devices with their start and end apart: 6 -> 3, of which waited for: 6 -> 1; matrix products, arithmetic and copies ran while one was open for 10% -> 8% of each run, Pallas kernels for 0% -> 17%
where the time goes in v1:
time: 274 us; the launch traced here: 273 us
  Pallas kernels  112 us (41%)
  blocking collectives  36.6 us (13%)
  matrix products  35.8 us (13%)
  waiting for transfers between devices  34.4 us (13%)
  other arithmetic  17.9 us (7%)
  between operations  14.8 us (5%)
  local copies, waits for them, and re-layouts  14.2 us (5%)
  starting transfers between devices  7.51 us (3%)
    pallas_call x1, Pallas kernels, combine(): pl.pallas_call(functools.partial(combine_kernel, groups), out_shape=jax.S...  44.1 us
    psum x1, blocking collectives, on_device(): lax.psum((grad_position_table, grad_gain_first, grad_gain_second, grad_ro...  36.6 us
    psum x1, waiting for transfers between devices, on_device(): lax.psum((grad_projections.astype(jnp.bfloat16), grad_attention_out.astyp...  34.3 us
    pallas_call x2, Pallas kernels, tensor_total(): pl.pallas_call(tensor_sum_kernel, out_shape=jax.ShapeDtypeStruct((rows, w...  30.4 us
    pallas_call x1, Pallas kernels, dispatch(): pl.pallas_call(functools.partial(dispatch_kernel, groups), out_shape=jax....  26.9 us
    unnamed x120, local copies, waits for them, and re-layouts  11.3 us
    pallas_call x2, Pallas kernels, local_call(): pl.pallas_call(kernel, out_shape=outs, in_specs=[vmem()] * len(args), out...  10.4 us
    dot_general x3, matrix products, columns_dot(): lax.dot_general(left, right, (((0,), (0,)), ((), ())), preferred_element_...  7.37 us
  transfers between devices with their start and end apart: 3, of which 1 were waited for; matrix products, arithmetic and copies ran while one was open for 8% of the time, Pallas kernels for 17%

profile of v1, /device:TPU:0, one launch (start us, length us, event | category | flops | bytes accessed | tf_op | source)
XLA Modules:
  0.0 273.0 jit_solution(17371939157266209973)
XLA Ops:
  10.9 2.3 convolution_convert_fusion.5
  13.2 7.3 %all-to-all-start = ((bf16[8,32,768]{2,1,0:T(8,128)(2,1)}), bf16[8,32,768]{2,1,0:T(8,128)(2,1)}, u32[]{:S(2)}, u32[]{:S(2)}) async-start(bf16[8,32,768]{2,1,0:T(8,128)(2,1)} %bitcast.21), calls=%async_computation | async-start | bytes 786432 | tf_op jit(solution)/shard_map/all_to_all | solution.py:210
  21.7 1.9 fusion.44
  24.5 4.9 %shard_map.204 = (bf16[512,192]{1,0:T(8,128)(2,1)S(1)}, f32[3,512,1]{2,1,0:T(8,128)S(1)}) custom-call(bf16[3,512,192]{2,1,0:T(8,128)(2,1)S(1)} %bitcast.85, f32[3,1024]{1,0:T(4,128)S(1)} %convolution_bitcast_fusion.2.line_ref, s32[512,1]{1,0:T(8,128)S(1)} %copy.50.column_ref, s32[1,512]{1,0:T(1,128)S(1)} %bitcast.89), custom_call_target="tpu_custom_call" | custom-call | flops 1000000000 | bytes 30000000 | tf_op jit(solution)/shard_map/pallas_call | solution.py:422
  29.9 15.2 %shard_map.205 = f32[512,768]{1,0:T(8,128)S(1)} custom-call(bf16[512,768]{1,0:T(8,128)(2,1)S(1)} %convolution_convert_fusion.3.x_ref), custom_call_target="tpu_custom_call" | custom-call | bytes 30000000 | tf_op jit(solution)/shard_map/pallas_call | solution.py:107
  49.9 26.9 %shard_map.206 = bf16[4,8,32,896]{3,2,1,0:T(8,128)(2,1)S(1)} custom-call(bf16[8,32,896]{2,1,0:T(8,128)(2,1)S(1)} %bitcast.87), custom_call_target="tpu_custom_call" | custom-call | bytes 50000000 | tf_op jit(solution)/shard_map/pallas_call | solution.py:213
  78.9 2.7 fusion.20
  81.6 1.6 copy-done.55
  83.2 3.1 %convolution_convert_fusion.1 = bf16[1024,768]{1,0:T(8,128)(2,1)} fusion(bf16[1,768,768]{2,1,0:T(8,128)(2,1)S(1)} %copy-done, f32[1024,768]{1,0:T(8,128)S(1)} %fusion.20), kind=kOutput, calls=%fused_computation.33 | convolution fusion | flops 1215823872 | bytes 5898240 | tf_op jit(solution)/shard_map/dot_general | solution.py:530
  86.4 1.9 multiply_convert_fusion
  88.8 4.3 %fusion.3 = bf16[1024,768]{1,0:T(8,128)(2,1)S(1)} fusion(f32[1024,768]{1,0:T(8,128)S(1)} %copy-done.56, bf16[1024,768]{1,0:T(8,128)(2,1)S(1)} %bitcast.92, bf16[1,768,768]{2,1,0:T(8,128)(2,1)S(1)} %copy-done), kind=kOutput, calls=%fused_computation.7 | convolution fusion | flops 1226833920 | bytes 7471104 | tf_op jit(solution)/shard_map/dot_general | solution.py:342
  95.0 44.1 %shard_map.207 = bf16[2,4,8,32,768]{4,3,2,1,0:T(8,128)(2,1)S(1)} custom-call(bf16[4,8,32,768]{3,2,1,0:T(8,128)(2,1)S(1)} %bitcast.83, bf16[4,8,32,768]{3,2,1,0:T(8,128)(2,1)S(1)} %bitcast.84), custom_call_target="tpu_custom_call" | custom-call | bytes 120000000 | tf_op jit(solution)/shard_map/pallas_call | solution.py:318
  143.5 1.9 multiply_reduce_fusion
  153.3 5.5 %shard_map.208 = (bf16[3,512,192]{2,1,0:T(8,128)(2,1)S(1)}, f32[3,1024]{1,0:T(4,128)S(1)}) custom-call(bf16[3,512,192]{2,1,0:T(8,128)(2,1)S(1)} %bitcast.86, f32[3,1024]{1,0:T(4,128)S(1)} %copy-done.6, s32[512,1]{1,0:T(8,128)S(1)} %copy.50.column_ref, s32[1,512]{1,0:T(1,128)S(1)} %bitcast.90, f32[3,512,1]{2,1,0:T(8,128)S(1)} %copy-done.9, ...), custom_call_target="tpu_custom_call" | custom-call | flops 1000000000 | bytes 30000000 | tf_op jit(solution)/shard_map/pallas_call | solution.py:422
  159.2 1.7 bitcast_convert_fusion.x_ref
  160.9 1.7 fusion.22
  164.6 15.2 %shard_map.209 = f32[512,768]{1,0:T(8,128)S(1)} custom-call(bf16[512,768]{1,0:T(8,128)(2,1)S(1)} %copy-done.4), custom_call_target="tpu_custom_call" | custom-call | bytes 30000000 | tf_op jit(solution)/shard_map/pallas_call | solution.py:107
  182.8 36.6 %all-reduce.1 = (f32[768]{0:T(1024)}, f32[32,3]{0,1:T(4,128)}, f32[768]{0:T(1024)}, f32[768,8]{0,1:T(8,128)}) all-reduce(f32[768]{0:T(1024)S(1)} %get-tuple-element.20, f32[32,3]{0,1:T(4,128)S(1)} %fusion.46, f32[768]{0:T(1024)S(1)} %copy-done.46, f32[768,8]{0,1:T(8,128)S(1)} %copy-done.26), channel_id=1, replica_groups=mesh['expert'=8,'tensor'=4] {'expert'}, use_global_device_ids=true, to_apply=%region_16.17 | all-reduce | flops 7776 | bytes 62208 | tf_op jit(solution)/shard_map/psum | solution.py:582
  219.4 1.9 fusion.6
  221.3 2.9 %convolution_bitcast_fusion.1 = f32[1,768,768]{2,1,0:T(8,128)} fusion(bf16[1024,768]{1,0:T(8,128)(2,1)S(1)} %copy-done.59, bf16[1024,896]{1,0:T(8,128)(2,1)S(1)} %bitcast.82), kind=kOutput, calls=%fused_computation.31 | convolution fusion | flops 1207959552 | bytes 5505024 | tf_op jit(solution)/shard_map/dot_general | solution.py:348
  224.2 3.3 %convolution_bitcast_fusion = f32[1,768,768]{2,1,0:T(8,128)} fusion(bf16[1024,768]{1,0:T(8,128)(2,1)S(1)} %fusion.6, f32[1024,768]{1,0:T(8,128)S(1)} %copy-done.57), kind=kOutput, calls=%fused_computation.30 | convolution fusion | flops 1215037440 | bytes 7077888 | tf_op jit(solution)/shard_map/dot_general | solution.py:348
  227.5 34.3 %all-reduce.5.cloned.1.call-done = (bf16[3,768,192]{1,2,0:T(8,128)(2,1)}, bf16[192,768]{1,0:T(8,128)(2,1)}) async-done(((bf16[3,768,192]{1,2,0:T(8,128)(2,1)}, bf16[192,768]{1,0:T(8,128)(2,1)}), (bf16[3,768,192]{1,2,0:T(8,128)(2,1)}, bf16[192,768]{1,0:T(8,128)(2,1)})) %all-reduce.5.cloned.1.call-update) | async-done | bytes 1179664 | tf_op jit(solution)/shard_map/psum | solution.py:579
  261.8 1.8 convert_element_type.133
  263.6 2.5 convert_element_type.131
  (172 shorter events, 32.7 us)
Async XLA Ops:
  7.2 76.1 %copy-start = (bf16[1,768,768]{2,1,0:T(8,128)(2,1)S(1)}, bf16[1,768,768]{2,1,0:T(8,128)(2,1)}, u32[]{:S(2)}) copy-start(bf16[1,768,768]{2,1,0:T(8,128)(2,1)} %param.23) | copy-start | bytes 3538948
  7.2 13.8 %copy-start.50 = (s32[15]{0:T(128)S(1)}, s32[15]{0:T(128)}, u32[]{:S(2)}) copy-start(s32[15]{0:T(128)} %constant.81.clone) | copy-start | bytes 184
  7.2 13.3 %copy-start.54 = (s32[1,4]{1,0:T(1,128)S(1)}, s32[1,4]{1,0:T(1,128)}, u32[]{:S(2)}) copy-start(s32[1,4]{1,0:T(1,128)} %param.14) | copy-start | bytes 52
  7.2 13.6 %copy-start.14 = (bf16[512,768]{1,0:T(8,128)(2,1)S(1)}, bf16[512,768]{1,0:T(8,128)(2,1)}, u32[]{:S(2)}) copy-start(bf16[512,768]{1,0:T(8,128)(2,1)} %param.13) | copy-start | bytes 2359300
  8.1 13.7 %copy-start.44 = (f32[768]{0:T(1024)S(1)}, f32[768]{0:T(1024)}, u32[]{:S(2)}) copy-start(f32[768]{0:T(1024)} %param.16) | copy-start | bytes 9220
  10.2 10.9 %copy-start.39 = (s32[512]{0:T(512)}, s32[512]{0:T(512)S(1)}, u32[]{:S(2)}) copy-start(s32[512]{0:T(512)S(1)} %fusion.49) | copy-start | bytes 6148
  13.2 32.9 %all-to-all-start = ((bf16[8,32,768]{2,1,0:T(8,128)(2,1)}), bf16[8,32,768]{2,1,0:T(8,128)(2,1)}, u32[]{:S(2)}, u32[]{:S(2)}) async-start(bf16[8,32,768]{2,1,0:T(8,128)(2,1)} %bitcast.21), calls=%async_computation | async-start | bytes 786432 | tf_op jit(solution)/shard_map/all_to_all | solution.py:210
  20.4 66.0 %all-gather.3.cloned.1.call-start = ((), (), s32[]{:S(2)}) async-start(), calls=%async_computation.1 | async-start | bytes 1966080 | tf_op jit(solution)/shard_map/all_gather | solution.py:211
  21.0 2.6 copy-start.35
  21.6 2.5 copy-start.47
  24.3 5.1 %copy-start.2 = (bf16[512,3,192]{2,0,1:T(8,128)(2,1)}, bf16[512,3,192]{2,0,1:T(8,128)(2,1)S(1)}, u32[]{:S(2)}) copy-start(bf16[512,3,192]{2,0,1:T(8,128)(2,1)S(1)} %copy.49) | copy-start | bytes 1769476
  24.5 5.0 %copy-start.5 = (f32[3,1024]{1,0:T(4,128)}, f32[3,1024]{1,0:T(4,128)S(1)}, u32[]{:S(2)}) copy-start(f32[3,1024]{1,0:T(4,128)S(1)} %convolution_bitcast_fusion.2.line_ref) | copy-start | bytes 36868
  24.5 5.0 %copy-start.21 = (bf16[192,768]{1,0:T(8,128)(2,1)S(1)}, bf16[192,768]{1,0:T(8,128)(2,1)}, u32[]{:S(2)}) copy-start(bf16[192,768]{1,0:T(8,128)(2,1)} %param.18) | copy-start | bytes 884740
  29.5 15.6 %copy-start.8 = (f32[3,512,1]{2,1,0:T(8,128)}, f32[3,512,1]{2,1,0:T(8,128)S(1)}, u32[]{:S(2)}) copy-start(f32[3,512,1]{2,1,0:T(8,128)S(1)} %get-tuple-element.15.log_ref) | copy-start | bytes 18436
  29.5 15.6 %copy-start.15 = (bf16[512,768]{1,0:T(8,128)(2,1)S(1)}, bf16[512,768]{1,0:T(8,128)(2,1)}, u32[]{:S(2)}) copy-start(bf16[512,768]{1,0:T(8,128)(2,1)} %param.13) | copy-start | bytes 2359300
  46.1 215.8 %all-reduce.5.cloned.1.call-start = ((), (), s32[]{:S(2)}) async-start(), calls=%async_computation.2 | async-start | bytes 2359296 | tf_op jit(solution)/shard_map/psum | solution.py:579
  86.4 2.4 copy-start.56
  88.8 4.3 %copy-start.51 = (bf16[1,768,768]{2,1,0:T(8,128)(2,1)S(1)}, bf16[1,768,768]{2,1,0:T(8,128)(2,1)}, u32[]{:S(2)}) copy-start(bf16[1,768,768]{2,1,0:T(8,128)(2,1)} %param.22) | copy-start | bytes 3538948
  140.3 2.3 copy-start.28
  153.3 5.5 %copy-start.52 = (bf16[3,768,192]{1,2,0:T(8,128)(2,1)S(1)}, bf16[3,768,192]{1,2,0:T(8,128)(2,1)}, u32[]{:S(2)}) copy-start(bf16[3,768,192]{1,2,0:T(8,128)(2,1)} %param.17) | copy-start | bytes 2654212
  158.8 2.0 copy-start.7
  158.9 2.0 copy-start.16
  164.6 15.2 %copy-start.17 = (bf16[512,768]{1,0:T(8,128)(2,1)S(1)}, bf16[512,768]{1,0:T(8,128)(2,1)}, u32[]{:S(2)}) copy-start(bf16[512,768]{1,0:T(8,128)(2,1)} %param.13) | copy-start | bytes 2359300
  221.3 2.9 %copy-start.57 = (f32[1024,768]{1,0:T(8,128)S(1)}, f32[1024,768]{1,0:T(8,128)}, u32[]{:S(2)}) copy-start(f32[1024,768]{1,0:T(8,128)} %copy-done.55) | copy-start | bytes 9437188
  (39 other events, 49.5 us)
Sparse Core Ops, SparseCore 0:
  46.2 28.4 all-gather.2
  182.9 78.8 all-reduce.4

commit v2 on v1

--- a/solution.py
+++ b/solution.py
@@ -10,6 +10,7 @@
 edge_list = (1, 2, 3, 4, 5, 6, 7, 8, 12, 16, 23, 32, 46, 64, 91)
 tiny_eps = 1e-06
 masked_score = -1e30
+sum_chunks = 4
 largest_logit = lax.Precision.HIGHEST
 
 
@@ -78,44 +79,70 @@
     )
 
 
-def tensor_sum_kernel(x_ref, o_ref, near, chip, far, send_sem, recv_sem):
+def tensor_sum_steps(x_ref, o_ref, near, chip, far, send_sem, recv_sem):
     _, core, _, sibling, across = tensor_places()
     half = x_ref.shape[0] // 2
+    chunk = half // sum_chunks
+    copies = []
+
+    def rows_of(which, turn):
+        return pl.ds(pl.multiple_of(which * half + turn * chunk, chunk), chunk)
+
+    def begin(source, target, place, device):
+        copy = remote(source, target, send_sem.at[place], recv_sem.at[place], {"tensor": device})
+        copy.start()
+        copies.append(copy)
+        return copy
+
+    first = [
+        begin(x_ref.at[rows_of(1 - core, turn)], near.at[turn], turn, sibling)
+        for turn in range(sum_chunks)
+    ]
+    yield
+    second = []
+    for turn in range(sum_chunks):
+        first[turn].wait_recv()
+        own = x_ref[rows_of(core, turn)].astype(jnp.float32)
+        chip[turn] = (own + near[turn].astype(jnp.float32)).astype(chip.dtype)
+        second.append(begin(chip.at[turn], far.at[turn], sum_chunks + turn, across))
+    yield
+    third = []
+    for turn in range(sum_chunks):
+        second[turn].wait_recv()
+        own = rows_of(core, turn)
+        o_ref[own] = chip[turn].astype(jnp.float32) + far[turn].astype(jnp.float32)
+        third.append(begin(o_ref.at[own], o_ref.at[own], 2 * sum_chunks + turn, sibling))
+    yield
+    for copy in third:
+        copy.wait_recv()
+    for copy in copies:
+        copy.wait_send()
+    yield
+
+
+def tensor_sum_scratch(rows, width):
+    chunk = pltpu.VMEM((sum_chunks, rows // 2 // sum_chunks, width), jnp.bfloat16)
+    sems = pltpu.SemaphoreType.DMA((3 * sum_chunks,))
+    return [chunk, chunk, chunk, sems, sems]
+
+
+def tensor_sum_kernel(*refs):
+    _, _, _, sibling, across = tensor_places()
     greet([{"tensor": sibling}, {"tensor": across}])
-    own = pl.ds(pl.multiple_of(core * half, half), half)
-    other = pl.ds(pl.multiple_of((1 - core) * half, half), half)
-    first = remote(x_ref.at[other], near, send_sem.at[0], recv_sem.at[0], {"tensor": sibling})
-    first.start()
-    first.wait()
-    chip[...] = (x_ref[own].astype(jnp.float32) + near[...].astype(jnp.float32)).astype(chip.dtype)
-    second = remote(chip, far, send_sem.at[1], recv_sem.at[1], {"tensor": across})
-    second.start()
-    second.wait()
-    o_ref[own] = chip[...].astype(jnp.float32) + far[...].astype(jnp.float32)
-    third = remote(
-        o_ref.at[own], o_ref.at[own], send_sem.at[2], recv_sem.at[2], {"tensor": sibling}
-    )
-    third.start()
-    third.wait()
+    for _ in tensor_sum_steps(*refs):
+        pass
 
 
 def tensor_total(value, collective_id):
     rows, width = value.shape
-    if lax.axis_size("tensor") != 4 or rows % 32:
+    if lax.axis_size("tensor") != 4 or rows % (32 * sum_chunks):
         return lax.psum(value, "tensor")
-    half = pltpu.VMEM((rows // 2, width), jnp.bfloat16)
     return pl.pallas_call(
         tensor_sum_kernel,
         out_shape=jax.ShapeDtypeStruct((rows, width), jnp.float32),
         in_specs=[vmem()],
         out_specs=vmem(),
-        scratch_shapes=[
-            half,
-            half,
-            half,
-            pltpu.SemaphoreType.DMA((3,)),
-            pltpu.SemaphoreType.DMA((3,)),
-        ],
+        scratch_shapes=tensor_sum_scratch(rows, width),
         compiler_params=pltpu.CompilerParams(
             collective_id=collective_id, has_side_effects=True, vmem_limit_bytes=32 * 2**20
         ),
@@ -338,6 +365,150 @@
     )(ahead, back)
 
 
+def finish_kernel(
+    groups, x_ref, unit_ref, big_ref, small_ref, o_ref, big_out, small_out, gain_out, *scratch
+):
+    (
+        pair_buf,
+        line_send,
+        line_buf,
+        small_buf,
+        gain_buf,
+        pair_sems,
+        line_sems,
+        spread_sems,
+        pass_sems,
+        small_sems,
+        gain_sems,
+    ) = scratch[:11]
+    here = lax.axis_index("expert")
+    _, _, _, sibling, across = tensor_places()
+    lines = groups // 2
+    place = here // 2
+    lane = here % 2
+    pair = place * 2 + (1 - lane)
+    peers = [lax.rem(here + step, groups) for step in range(groups)]
+    greet([{"expert": peer} for peer in peers[1:]] + [{"tensor": sibling}, {"tensor": across}])
+    copies = []
+
+    def begin(source, target, sems, index, device):
+        copy = remote(source, target, sems.at[0, index], sems.at[1, index], {"expert": device})
+        copy.start()
+        copies.append(copy)
+        return copy
+
+    order = list(range(1, lines)) + [0]
+    places = [lax.rem(place + step, lines) for step in range(lines)]
+    pairs = {}
+    for step in order:
+        pairs[step] = begin(
+            big_ref.at[places[step] * 2 + (1 - lane)], pair_buf.at[step], pair_sems, step, pair
+        )
+    steps = tensor_sum_steps(x_ref, o_ref, *scratch[11:])
+    next(steps)
+    smalls = [None]
+    small_buf[here] = small_ref[...]
+    for step in range(1, groups):
+        smalls.append(
+            begin(small_ref, small_buf.at[here], small_sems, step, peers[step])
+        )
+    next(steps)
+    along = {}
+    for step in order:
+        pairs[step].wait_recv()
+        line_send[step] = (
+            big_ref[places[step] * 2 + lane].astype(jnp.float32)
+            + pair_buf[step].astype(jnp.float32)
+        ).astype(line_send.dtype)
+        if step:
+            along[step] = begin(
+                line_send.at[step], line_buf.at[step], line_sems, step, places[step] * 2 + lane
+            )
+    next(steps)
+    next(steps)
+    gain = jnp.sum(o_ref[...] * unit_ref[...], axis=0, keepdims=True)
+    gain_out[...] = jnp.broadcast_to(gain, gain_out.shape)
+    gain_buf[here] = gain_out[...]
+    gains = [None]
+    for step in range(1, groups):
+        gains.append(begin(gain_out, gain_buf.at[here], gain_sems, step, peers[step]))
+    total = line_send[0].astype(jnp.float32)
+    for step in range(1, lines):
+        along[step].wait_recv()
+        total = total + line_buf[step].astype(jnp.float32)
+    big_out[here] = total.astype(big_out.dtype)
+    spread = {}
+    for step in order:
+        device = places[step] * 2 + lane if step else pair
+        spread[step] = begin(big_out.at[here], big_out.at[here], spread_sems, step, device)
+    passed = []
+    for step in range(1, lines):
+        spread[step].wait_recv()
+        came = lax.rem(place + lines - step, lines) * 2 + lane
+        passed.append(begin(big_out.at[came], big_out.at[came], pass_sems, step, pair))
+    for copy in smalls[1:] + gains[1:] + [spread[0]] + passed:
+        copy.wait_recv()
+    for copy in copies:
+        copy.wait_send()
+    small_sum = small_buf[0]
+    gain_sum = gain_buf[0]
+    for source in range(1, groups):
+        small_sum = small_sum + small_buf[source]
+        gain_sum = gain_sum + gain_buf[source]
+    small_out[...] = small_sum
+    gain_out[...] = gain_sum
+
+
+def finish(partial, unit, large, small, collective_id):
+    rows, width = partial.shape
+    groups = lax.axis_size("expert")
+    if (
+        lax.axis_size("tensor") != 4
+        or groups != 8
+        or large.shape[0] % (16 * groups)
+        or rows % (32 * sum_chunks)
+    ):
+        total = lax.psum(partial, "tensor")
+        gain, small = lax.psum((jnp.sum(total * unit, axis=0), small), "expert")
+        large = lax.psum(large.astype(jnp.bfloat16), "expert")
+        return total, large.astype(jnp.float32), small, gain
+    piece = (large.shape[0] // groups, width)
+    lines = groups // 2
+    few = pltpu.SemaphoreType.DMA((2, lines))
+    many = pltpu.SemaphoreType.DMA((2, groups))
+    gains = (8, width)
+    total, large, small, gain = pl.pallas_call(
+        functools.partial(finish_kernel, groups),
+        out_shape=(
+            jax.ShapeDtypeStruct((rows, width), jnp.float32),
+            jax.ShapeDtypeStruct((groups,) + piece, jnp.bfloat16),
+            jax.ShapeDtypeStruct(small.shape, jnp.float32),
+            jax.ShapeDtypeStruct(gains, jnp.float32),
+        ),
+        in_specs=[vmem()] * 4,
+        out_specs=(vmem(),) * 4,
+        scratch_shapes=[
+            pltpu.VMEM((lines,) + piece, jnp.bfloat16),
+            pltpu.VMEM((lines,) + piece, jnp.bfloat16),
+            pltpu.VMEM((lines,) + piece, jnp.bfloat16),
+            pltpu.VMEM((groups,) + small.shape, jnp.float32),
+            pltpu.VMEM((groups,) + gains, jnp.float32),
+            few,
+            few,
+            few,
+            few,
+            many,
+            many,
+        ]
+        + tensor_sum_scratch(rows, width),
+        compiler_params=pltpu.CompilerParams(
+            collective_id=collective_id, has_side_effects=True, vmem_limit_bytes=40 * 2**20
+        ),
+        cost_estimate=pl.CostEstimate(flops=0, bytes_accessed=100_000_000, transcendentals=0),
+    )(partial.astype(jnp.bfloat16), unit, large.astype(jnp.bfloat16).reshape((groups,) + piece), small)
+    return total, large.astype(jnp.float32).reshape(-1, width), small, gain[0]
+
+
 def rows_dot(left, right):
     return lax.dot_general(
         left, right, (((1,), (1,)), ((), ())), preferred_element_type=jnp.float32
@@ -568,29 +739,35 @@
         "hm,bm->bh", offset_sums, bucket_pick, precision=largest_logit
     )
     grad_projections = jnp.einsum(
-        "nd,cnh->cdh", normed_first, grad_projected, preferred_element_type=jnp.float32
-    )
-    grad_normed_first = tensor_total(
+        "cnh,nd->chd", grad_projected, normed_first, preferred_element_type=jnp.float32
+    ).reshape(3 * width_here, model_width)
+    first_scale = lax.rsqrt(
+        jnp.mean(token_float * token_float, axis=-1, keepdims=True) + tiny_eps
+    )
+    table_row = jnp.pad(
+        grad_position_table.reshape(1, -1),
+        ((0, 0), (0, model_width - buckets_total * heads_here)),
+    )
+    small = jnp.concatenate([grad_gain_second[None], table_row, grad_router.T], axis=0)
+    small = jnp.pad(small, ((0, -small.shape[0] % 16), (0, 0)))
+    grad_normed_first, large, small, grad_gain_first = finish(
         jnp.einsum("cnh,cdh->nd", grad_projected, projections, preferred_element_type=jnp.float32),
+        token_float * first_scale,
+        jnp.concatenate([grad_projections, grad_attention_out], axis=0),
+        small,
         3,
     )
-    grad_first_in, grad_gain_first = first_back(grad_normed_first)
+    grad_first_in = first_back(grad_normed_first)[0]
     grad_tokens = grad_residual + grad_first_in
-    large = lax.psum(
-        (grad_projections.astype(jnp.bfloat16), grad_attention_out.astype(jnp.bfloat16)), "expert"
-    )
-    small = lax.psum(
-        (grad_position_table, grad_gain_first, grad_gain_second, grad_router), "expert"
-    )
     return (
         layer_output,
         grad_tokens,
-        small[1],
-        large[0].astype(jnp.float32),
-        large[1].astype(jnp.float32),
+        grad_gain_first,
+        large[: 3 * width_here].reshape(3, width_here, model_width).transpose(0, 2, 1),
+        large[3 * width_here :],
+        small[1, : buckets_total * heads_here].reshape(buckets_total, heads_here),
         small[0],
-        small[2],
-        small[3],
+        small[2 : 2 + experts_total].T,
         grad_expert_in,
         grad_expert_out,
     )

time: 274 us -> 237 us (0.86)
  blocking collectives: 36.6 us -> 0 us
  waiting for transfers between devices: 34.4 us -> 0.02 us
  Pallas kernels: 112 us -> 142 us
  local copies, waits for them, and re-layouts: 14.2 us -> 22.1 us
  other arithmetic: 17.9 us -> 15.1 us
    pallas_call x0 -> x1, Pallas kernels: none -> 47.8 us  [finish(): pl.pallas_call(functools.partial(finish_kernel, groups), out_shape=(jax.S...]
    psum x1 -> x0, blocking collectives: 36.6 us -> none  [on_device(): lax.psum((grad_position_table, grad_gain_first, grad_gain_second, grad_ro...]
    psum x1 -> x0, waiting for transfers between devices: 34.3 us -> none  [on_device(): lax.psum((grad_projections.astype(jnp.bfloat16), grad_attention_out.astyp...]
    pallas_call x2 -> x1, Pallas kernels: 30.4 us -> 14 us  [tensor_total(): pl.pallas_call(tensor_sum_kernel, out_shape=jax.ShapeDtypeStruct((rows, w...]
    convert_element_type x2 -> x0, other arithmetic: 4.33 us -> none  [the longest x1 2.52 us: on_device(): large[0].astype(jnp.float32)]
    slice x1 -> x5, local copies, waits for them, and re-layouts: 0.21 us -> 3.06 us  [the longest x1 1.36 us: on_device(): large[:3 * width_here].reshape(3, width_here, model_width)]
    unnamed x120 -> x87, local copies, waits for them, and re-layouts: 11.3 us -> 13.6 us
  transfers between devices with their start and end apart: 3 -> 2, of which waited for: 1 -> 0; matrix products, arithmetic and copies ran while one was open for 8% -> 7% of each run, Pallas kernels for 17% -> 19%
where the time goes in v2:
time: 237 us; the launch traced here: 236 us
  Pallas kernels  142 us (60%)
  matrix products  35.2 us (15%)
  local copies, waits for them, and re-layouts  22.1 us (9%)
  other arithmetic  15.1 us (6%)
  between operations  14.6 us (6%)
  starting transfers between devices  7.29 us (3%)
    pallas_call x1, Pallas kernels, finish(): pl.pallas_call(functools.partial(finish_kernel, groups), out_shape=(jax.S...  47.8 us
    pallas_call x1, Pallas kernels, combine(): pl.pallas_call(functools.partial(combine_kernel, groups), out_shape=jax.S...  44.2 us
    pallas_call x1, Pallas kernels, dispatch(): pl.pallas_call(functools.partial(dispatch_kernel, groups), out_shape=jax....  25.4 us
    pallas_call x1, Pallas kernels, tensor_total(): pl.pallas_call(tensor_sum_kernel, out_shape=jax.ShapeDtypeStruct((rows, w...  14 us
    unnamed x87, local copies, waits for them, and re-layouts  13.6 us
    pallas_call x2, Pallas kernels, local_call(): pl.pallas_call(kernel, out_shape=outs, in_specs=[vmem()] * len(args), out...  10.6 us
    dot_general x3, matrix products, columns_dot(): lax.dot_general(left, right, (((0,), (0,)), ((), ())), preferred_element_...  7.37 us
    all_to_all x1, starting transfers between devices, dispatch(): lax.all_to_all(send, 'expert', split_axis=0, concat_axis=0, tiled=True)  7.25 us
  transfers between devices with their start and end apart: 2, of which 0 were waited for; matrix products, arithmetic and copies ran while one was open for 7% of the time, Pallas kernels for 19%

profile of v2, /device:TPU:0, one launch (start us, length us, event | category | flops | bytes accessed | tf_op | source)
XLA Modules:
  0.0 236.4 jit_solution(11121143005914494818)
XLA Ops:
  10.9 2.3 convolution_convert_fusion.5
  13.2 7.3 %all-to-all-start = ((bf16[8,32,768]{2,1,0:T(8,128)(2,1)}), bf16[8,32,768]{2,1,0:T(8,128)(2,1)S(1)}, u32[]{:S(2)}, u32[]{:S(2)}) async-start(bf16[8,32,768]{2,1,0:T(8,128)(2,1)} %bitcast.21), calls=%async_computation | async-start | bytes 786432 | tf_op jit(solution)/shard_map/all_to_all | solution.py:237
  21.3 2.0 fusion.36
  24.2 4.9 %shard_map.204 = (bf16[512,192]{1,0:T(8,128)(2,1)S(1)}, f32[3,512,1]{2,1,0:T(8,128)S(1)}) custom-call(bf16[3,512,192]{2,1,0:T(8,128)(2,1)S(1)} %bitcast.92, f32[3,1024]{1,0:T(4,128)S(1)} %convolution_bitcast_fusion.2.line_ref, s32[512,1]{1,0:T(8,128)S(1)} %copy.58.column_ref, s32[1,512]{1,0:T(1,128)S(1)} %bitcast.96), custom_call_target="tpu_custom_call" | custom-call | flops 1000000000 | bytes 30000000 | tf_op jit(solution)/shard_map/pallas_call | solution.py:593
  29.5 14.0 %shard_map.205 = f32[512,768]{1,0:T(8,128)S(1)} custom-call(bf16[512,768]{1,0:T(8,128)(2,1)S(1)} %convolution_convert_fusion.3.refs_0_), custom_call_target="tpu_custom_call" | custom-call | bytes 30000000 | tf_op jit(solution)/shard_map/pallas_call | solution.py:140
  43.5 1.5 multiply_reduce_fusion.2
  45.8 1.6 multiply_convert_fusion.2
  49.0 1.6 convolution_convert_fusion.4
  50.6 25.4 %shard_map.206 = bf16[4,8,32,896]{3,2,1,0:T(8,128)(2,1)S(1)} custom-call(bf16[8,32,896]{2,1,0:T(8,128)(2,1)S(1)} %bitcast.94), custom_call_target="tpu_custom_call" | custom-call | bytes 50000000 | tf_op jit(solution)/shard_map/pallas_call | solution.py:240
  77.4 3.1 %fusion.16 = f32[1024,768]{1,0:T(8,128)S(1)} fusion(bf16[1024,896]{1,0:T(8,128)(2,1)} %bitcast.88, bf16[1,768,768]{2,1,0:T(8,128)(2,1)} %param.22), kind=kOutput, calls=%fused_computation.47 | convolution fusion | flops 1207959552 | bytes 5898240 | tf_op jit(solution)/shard_map/dot_general | solution.py:698
  80.5 1.7 copy-done.40
  82.2 3.1 %convolution_convert_fusion.1 = bf16[1024,768]{1,0:T(8,128)(2,1)} fusion(bf16[1,768,768]{2,1,0:T(8,128)(2,1)S(1)} %copy-done, f32[1024,768]{1,0:T(8,128)S(1)} %fusion.16), kind=kOutput, calls=%fused_computation.31 | convolution fusion | flops 1215823872 | bytes 5898240 | tf_op jit(solution)/shard_map/dot_general | solution.py:701
  85.4 1.9 multiply_convert_fusion
  87.7 4.2 %fusion.3 = bf16[1024,768]{1,0:T(8,128)(2,1)S(1)} fusion(f32[1024,768]{1,0:T(8,128)S(1)} %copy-done.41, bf16[1024,768]{1,0:T(8,128)(2,1)S(1)} %bitcast.100, bf16[1,768,768]{2,1,0:T(8,128)(2,1)S(1)} %copy-done), kind=kOutput, calls=%fused_computation.7 | convolution fusion | flops 1226833920 | bytes 7471104 | tf_op jit(solution)/shard_map/dot_general | solution.py:513
  92.0 2.9 %convolution_bitcast_fusion.1 = f32[1,768,768]{2,1,0:T(8,128)} fusion(bf16[1024,768]{1,0:T(8,128)(2,1)S(1)} %fusion.3, bf16[1024,896]{1,0:T(8,128)(2,1)S(1)} %bitcast.89), kind=kOutput, calls=%fused_computation.29 | convolution fusion | flops 1207959552 | bytes 5505024 | tf_op jit(solution)/shard_map/dot_general | solution.py:519
  96.3 44.2 %shard_map.207 = bf16[2,4,8,32,768]{4,3,2,1,0:T(8,128)(2,1)S(1)} custom-call(bf16[4,8,32,768]{3,2,1,0:T(8,128)(2,1)S(1)} %bitcast.90, bf16[4,8,32,768]{3,2,1,0:T(8,128)(2,1)S(1)} %bitcast.91), custom_call_target="tpu_custom_call" | custom-call | bytes 120000000 | tf_op jit(solution)/shard_map/pallas_call | solution.py:345
  144.7 1.9 multiply_reduce_fusion
  150.3 1.8 copy.61.up_ref
  155.9 5.7 %shard_map.208 = (bf16[3,512,192]{2,1,0:T(8,128)(2,1)S(1)}, f32[3,1024]{1,0:T(4,128)S(1)}) custom-call(bf16[3,512,192]{2,1,0:T(8,128)(2,1)S(1)} %bitcast.93, f32[3,1024]{1,0:T(4,128)S(1)} %copy-done.10, s32[512,1]{1,0:T(8,128)S(1)} %copy-done.8, s32[1,512]{1,0:T(1,128)S(1)} %bitcast.97, f32[3,512,1]{2,1,0:T(8,128)S(1)} %copy-done.12, ...), custom_call_target="tpu_custom_call" | custom-call | flops 1000000000 | bytes 30000000 | tf_op jit(solution)/shard_map/pallas_call | solution.py:593
  162.8 1.6 convolution_convert_fusion.2
  169.2 47.8 %shard_map.209 = (f32[512,768]{1,0:T(8,128)S(1)}, bf16[8,96,768]{2,1,0:T(8,128)(2,1)S(1)}, f32[16,768]{1,0:T(8,128)S(1)}, f32[8,768]{1,0:T(8,128)S(1)}) custom-call(bf16[512,768]{1,0:T(8,128)(2,1)S(1)} %bitcast_convert_fusion.x_ref, f32[512,768]{1,0:T(8,128)S(1)} %get-tuple-element.84.unit_ref, bf16[8,96,768]{2,1,0:T(8,128)(2,1)S(1)} %bitcast.86, ...), custom_call_target="tpu_custom_call" | custom-call | bytes 100000000 | tf_op jit(solution)/shard_map/pallas_call | solution.py:480
  220.9 1.6 copy-done.42
  222.5 3.3 %convolution_bitcast_fusion = f32[1,768,768]{2,1,0:T(8,128)} fusion(bf16[1024,768]{1,0:T(8,128)(2,1)S(1)} %fusion.6, f32[1024,768]{1,0:T(8,128)S(1)} %copy-done.42), kind=kOutput, calls=%fused_computation.28 | convolution fusion | flops 1215037440 | bytes 7077888 | tf_op jit(solution)/shard_map/dot_general | solution.py:519
  227.2 1.6 fusion.11
  (144 shorter events, 35.0 us)
Async XLA Ops:
  7.2 75.0 %copy-start = (bf16[1,768,768]{2,1,0:T(8,128)(2,1)S(1)}, bf16[1,768,768]{2,1,0:T(8,128)(2,1)}, u32[]{:S(2)}) copy-start(bf16[1,768,768]{2,1,0:T(8,128)(2,1)} %param.23) | copy-start | bytes 3538948
  7.2 13.8 %copy-start.35 = (s32[15]{0:T(128)S(1)}, s32[15]{0:T(128)}, u32[]{:S(2)}) copy-start(s32[15]{0:T(128)} %constant.82.clone) | copy-start | bytes 184
  7.2 13.3 %copy-start.39 = (s32[1,4]{1,0:T(1,128)S(1)}, s32[1,4]{1,0:T(1,128)}, u32[]{:S(2)}) copy-start(s32[1,4]{1,0:T(1,128)} %param.14) | copy-start | bytes 52
  7.2 13.5 %copy-start.16 = (bf16[512,768]{1,0:T(8,128)(2,1)S(1)}, bf16[512,768]{1,0:T(8,128)(2,1)}, u32[]{:S(2)}) copy-start(bf16[512,768]{1,0:T(8,128)(2,1)} %param.13) | copy-start | bytes 2359300
  8.1 13.2 %copy-start.30 = (f32[768]{0:T(1024)S(1)}, f32[768]{0:T(1024)}, u32[]{:S(2)}) copy-start(f32[768]{0:T(1024)} %param.16) | copy-start | bytes 9220
  13.2 31.9 %all-to-all-start = ((bf16[8,32,768]{2,1,0:T(8,128)(2,1)}), bf16[8,32,768]{2,1,0:T(8,128)(2,1)S(1)}, u32[]{:S(2)}, u32[]{:S(2)}) async-start(bf16[8,32,768]{2,1,0:T(8,128)(2,1)} %bitcast.21), calls=%async_computation | async-start | bytes 786432 | tf_op jit(solution)/shard_map/all_to_all | solution.py:237
  20.4 64.9 %all-gather.3.cloned.1.call-start = ((), (), s32[]{:S(2)}) async-start(), calls=%async_computation.1 | async-start | bytes 1966080 | tf_op jit(solution)/shard_map/all_gather | solution.py:238
  21.1 2.6 %copy-start.33 = (s32[1024]{0:T(1024)}, s32[1024]{0:T(1024)S(1)}, u32[]{:S(2)}) copy-start(s32[1024]{0:T(1024)S(1)} %select_add_fusion) | copy-start | bytes 12292
  21.3 2.9 %copy-start.7 = (s32[512,1]{1,0:T(8,128)}, s32[512,1]{1,0:T(8,128)S(1)}, u32[]{:S(2)}) copy-start(s32[512,1]{1,0:T(8,128)S(1)} %copy.58.column_ref) | copy-start | bytes 6148
  24.0 5.1 %copy-start.4 = (bf16[512,3,192]{2,0,1:T(8,128)(2,1)}, bf16[512,3,192]{2,0,1:T(8,128)(2,1)S(1)}, u32[]{:S(2)}) copy-start(bf16[512,3,192]{2,0,1:T(8,128)(2,1)S(1)} %copy.57) | copy-start | bytes 1769476
  24.1 5.0 %copy-start.9 = (f32[3,1024]{1,0:T(4,128)}, f32[3,1024]{1,0:T(4,128)S(1)}, u32[]{:S(2)}) copy-start(f32[3,1024]{1,0:T(4,128)S(1)} %convolution_bitcast_fusion.2.line_ref) | copy-start | bytes 36868
  24.2 5.0 %copy-start.25 = (bf16[192,768]{1,0:T(8,128)(2,1)S(1)}, bf16[192,768]{1,0:T(8,128)(2,1)}, u32[]{:S(2)}) copy-start(bf16[192,768]{1,0:T(8,128)(2,1)} %param.18) | copy-start | bytes 884740
  29.1 14.4 %copy-start.11 = (f32[3,512,1]{2,1,0:T(8,128)}, f32[3,512,1]{2,1,0:T(8,128)S(1)}, u32[]{:S(2)}) copy-start(f32[3,512,1]{2,1,0:T(8,128)S(1)} %get-tuple-element.19.log_ref) | copy-start | bytes 18436
  29.1 14.4 %copy-start.17 = (bf16[512,768]{1,0:T(8,128)(2,1)S(1)}, bf16[512,768]{1,0:T(8,128)(2,1)}, u32[]{:S(2)}) copy-start(bf16[512,768]{1,0:T(8,128)(2,1)} %param.13) | copy-start | bytes 2359300
  43.5 2.3 copy-start.29
  45.0 3.3 %copy-start.28 = (bf16[768,8]{0,1:T(8,128)(2,1)S(1)}, bf16[768,8]{0,1:T(8,128)(2,1)}, u32[]{:S(2)}) copy-start(bf16[768,8]{0,1:T(8,128)(2,1)} %param.21) | copy-start | bytes 36868
  45.8 2.9 %copy-start.27 = (s32[512,1]{0,1:T(1,128)S(1)}, s32[512,1]{0,1:T(1,128)}, u32[]{:S(2)}) copy-start(s32[512,1]{0,1:T(1,128)} %param.15) | copy-start | bytes 6148
  85.4 2.4 copy-start.41
  87.7 4.2 %copy-start.2 = (bf16[4,8,32,896]{3,2,1,0:T(8,128)(2,1)S(1)}, bf16[4,8,32,896]{3,2,1,0:T(8,128)(2,1)}, u32[]{:S(2)}) copy-start(bf16[4,8,32,896]{3,2,1,0:T(8,128)(2,1)} %copy-done.1) | copy-start | bytes 5505028
  91.9 2.9 %copy-start.36 = (bf16[1,768,768]{2,1,0:T(8,128)(2,1)S(1)}, bf16[1,768,768]{2,1,0:T(8,128)(2,1)}, u32[]{:S(2)}) copy-start(bf16[1,768,768]{2,1,0:T(8,128)(2,1)} %param.22) | copy-start | bytes 3538948
  149.2 2.9 %copy-start.5 = (bf16[512,3,192]{2,0,1:T(8,128)(2,1)S(1)}, bf16[512,3,192]{2,0,1:T(8,128)(2,1)}, u32[]{:S(2)}) copy-start(bf16[512,3,192]{2,0,1:T(8,128)(2,1)} %copy-done.4) | copy-start | bytes 1769476
  155.9 5.7 %copy-start.37 = (bf16[3,768,192]{1,2,0:T(8,128)(2,1)S(1)}, bf16[3,768,192]{1,2,0:T(8,128)(2,1)}, u32[]{:S(2)}) copy-start(bf16[3,768,192]{1,2,0:T(8,128)(2,1)} %param.17) | copy-start | bytes 2654212
  162.8 2.2 copy-start.34
  222.5 3.9 %copy-start.19 = (bf16[512,768]{1,0:T(8,128)(2,1)S(1)}, bf16[512,768]{1,0:T(8,128)(2,1)}, u32[]{:S(2)}) copy-start(bf16[512,768]{1,0:T(8,128)(2,1)} %param.13) | copy-start | bytes 2359300
  (21 other events, 26.4 us)
Sparse Core Ops, SparseCore 0:
  45.9 26.8 all-gather.2

commit v3 on v2

--- a/solution.py
+++ b/solution.py
@@ -233,7 +233,7 @@
 
 def dispatch(send, collective_id):
     groups, part, width = send.shape
-    if collective_id is None or not kernels_fit(part):
+    if not kernels_fit(part):
         received = lax.all_to_all(send, "expert", split_axis=0, concat_axis=0, tiled=True)
         return lax.all_gather(received, "tensor", axis=0, tiled=False)
     sems = pltpu.SemaphoreType.DMA((groups,))
@@ -366,20 +366,20 @@
 
 
 def finish_kernel(
-    groups, x_ref, unit_ref, big_ref, small_ref, o_ref, big_out, small_out, gain_out, *scratch
+    groups, x_ref, unit_ref, big_ref, small_ref, o_ref, big_out, small_out, *scratch
 ):
     (
         pair_buf,
         line_send,
         line_buf,
+        small_send,
+        small_pair,
         small_buf,
-        gain_buf,
         pair_sems,
         line_sems,
         spread_sems,
         pass_sems,
         small_sems,
-        gain_sems,
     ) = scratch[:11]
     here = lax.axis_index("expert")
     _, _, _, sibling, across = tensor_places()
@@ -387,8 +387,9 @@
     place = here // 2
     lane = here % 2
     pair = place * 2 + (1 - lane)
-    peers = [lax.rem(here + step, groups) for step in range(groups)]
-    greet([{"expert": peer} for peer in peers[1:]] + [{"tensor": sibling}, {"tensor": across}])
+    places = [lax.rem(place + step, lines) for step in range(lines)]
+    friends = [pair] + [places[step] * 2 + lane for step in range(1, lines)]
+    greet([{"expert": friend} for friend in friends] + [{"tensor": sibling}, {"tensor": across}])
     copies = []
 
     def begin(source, target, sems, index, device):
@@ -398,7 +399,6 @@
         return copy
 
     order = list(range(1, lines)) + [0]
-    places = [lax.rem(place + step, lines) for step in range(lines)]
     pairs = {}
     for step in order:
         pairs[step] = begin(
@@ -406,12 +406,6 @@
         )
     steps = tensor_sum_steps(x_ref, o_ref, *scratch[11:])
     next(steps)
-    smalls = [None]
-    small_buf[here] = small_ref[...]
-    for step in range(1, groups):
-        smalls.append(
-            begin(small_ref, small_buf.at[here], small_sems, step, peers[step])
-        )
     next(steps)
     along = {}
     for step in order:
@@ -427,11 +421,9 @@
     next(steps)
     next(steps)
     gain = jnp.sum(o_ref[...] * unit_ref[...], axis=0, keepdims=True)
-    gain_out[...] = jnp.broadcast_to(gain, gain_out.shape)
-    gain_buf[here] = gain_out[...]
-    gains = [None]
-    for step in range(1, groups):
-        gains.append(begin(gain_out, gain_buf.at[here], gain_sems, step, peers[step]))
+    last = lax.broadcasted_iota(jnp.int32, small_ref.shape, 0) == small_ref.shape[0] - 1
+    small_send[0] = jnp.where(last, gain, small_ref[...])
+    small_first = begin(small_send.at[0], small_pair, small_sems, 0, pair)
     total = line_send[0].astype(jnp.float32)
     for step in range(1, lines):
         along[step].wait_recv()
@@ -441,22 +433,26 @@
     for step in order:
         device = places[step] * 2 + lane if step else pair
         spread[step] = begin(big_out.at[here], big_out.at[here], spread_sems, step, device)
+    small_first.wait_recv()
+    small_send[1] = small_send[0] + small_pair[...]
+    small_buf[place] = small_send[1]
+    smalls = [
+        begin(small_send.at[1], small_buf.at[place], small_sems, step, friends[step])
+        for step in range(1, lines)
+    ]
     passed = []
     for step in range(1, lines):
         spread[step].wait_recv()
         came = lax.rem(place + lines - step, lines) * 2 + lane
         passed.append(begin(big_out.at[came], big_out.at[came], pass_sems, step, pair))
-    for copy in smalls[1:] + gains[1:] + [spread[0]] + passed:
+    for copy in smalls + [spread[0]] + passed:
         copy.wait_recv()
     for copy in copies:
         copy.wait_send()
     small_sum = small_buf[0]
-    gain_sum = gain_buf[0]
-    for source in range(1, groups):
+    for source in range(1, lines):
         small_sum = small_sum + small_buf[source]
-        gain_sum = gain_sum + gain_buf[source]
     small_out[...] = small_sum
-    gain_out[...] = gain_sum
 
 
 def finish(partial, unit, large, small, collective_id):
@@ -475,30 +471,27 @@
     piece = (large.shape[0] // groups, width)
     lines = groups // 2
     few = pltpu.SemaphoreType.DMA((2, lines))
-    many = pltpu.SemaphoreType.DMA((2, groups))
-    gains = (8, width)
-    total, large, small, gain = pl.pallas_call(
+    total, large, small = pl.pallas_call(
         functools.partial(finish_kernel, groups),
         out_shape=(
             jax.ShapeDtypeStruct((rows, width), jnp.float32),
             jax.ShapeDtypeStruct((groups,) + piece, jnp.bfloat16),
             jax.ShapeDtypeStruct(small.shape, jnp.float32),
-            jax.ShapeDtypeStruct(gains, jnp.float32),
         ),
         in_specs=[vmem()] * 4,
-        out_specs=(vmem(),) * 4,
+        out_specs=(vmem(),) * 3,
         scratch_shapes=[
             pltpu.VMEM((lines,) + piece, jnp.bfloat16),
             pltpu.VMEM((lines,) + piece, jnp.bfloat16),
             pltpu.VMEM((lines,) + piece, jnp.bfloat16),
-            pltpu.VMEM((groups,) + small.shape, jnp.float32),
-            pltpu.VMEM((groups,) + gains, jnp.float32),
+            pltpu.VMEM((2,) + small.shape, jnp.float32),
+            pltpu.VMEM(small.shape, jnp.float32),
+            pltpu.VMEM((lines,) + small.shape, jnp.float32),
             few,
             few,
             few,
             few,
-            many,
-            many,
+            few,
         ]
         + tensor_sum_scratch(rows, width),
         compiler_params=pltpu.CompilerParams(
@@ -506,7 +499,7 @@
         ),
         cost_estimate=pl.CostEstimate(flops=0, bytes_accessed=100_000_000, transcendentals=0),
     )(partial.astype(jnp.bfloat16), unit, large.astype(jnp.bfloat16).reshape((groups,) + piece), small)
-    return total, large.astype(jnp.float32).reshape(-1, width), small, gain[0]
+    return total, large.astype(jnp.float32).reshape(-1, width), small, small[-1]
 
 
 def rows_dot(left, right):
@@ -647,7 +640,20 @@
         picked_rows = jnp.dot(send_pick, rows, preferred_element_type=jnp.float32)
         return picked_rows.astype(jnp.bfloat16).reshape(experts_total, part, rows.shape[1])
 
-    upstream_rows = dispatch(placed_rows(cotangent), None)
+    slot_pick = (
+        jnp.arange(experts_total * capacity, dtype=jnp.int32)[:, None]
+        == (route_column * capacity + slot)[None, :]
+    ).astype(jnp.bfloat16)
+    upstream_slots = (
+        jnp.dot(slot_pick, cotangent, preferred_element_type=jnp.float32)
+        .astype(jnp.bfloat16)
+        .reshape(experts_total, capacity, model_width)
+    )
+    upstream_rows = (
+        lax.all_to_all(upstream_slots, "expert", split_axis=0, concat_axis=0, tiled=True)
+        .reshape(experts_total, tensor_size, part, model_width)
+        .transpose(1, 0, 2, 3)
+    )
 
     token_float = tokens.astype(jnp.float32)
     normed_float, first_back = jax.vjp(rms_scale, token_float, gain_first)
@@ -749,7 +755,7 @@
         ((0, 0), (0, model_width - buckets_total * heads_here)),
     )
     small = jnp.concatenate([grad_gain_second[None], table_row, grad_router.T], axis=0)
-    small = jnp.pad(small, ((0, -small.shape[0] % 16), (0, 0)))
+    small = jnp.pad(small, ((0, 1 + (-small.shape[0] - 1) % 16), (0, 0)))
     grad_normed_first, large, small, grad_gain_first = finish(
         jnp.einsum("cnh,cdh->nd", grad_projected, projections, preferred_element_type=jnp.float32),
         token_float * first_scale,

time: 237 us -> 219 us (0.924); the launches traced: 236 us -> 215 us
  between operations: 14.6 us -> 1.21 us
  Pallas kernels: 142 us -> 138 us
  local copies, waits for them, and re-layouts: 22.1 us -> 19.6 us
    pallas_call x1, Pallas kernels: 47.8 us -> 41.6 us  [finish(): pl.pallas_call(functools.partial(finish_kernel, groups), out_shape=(jax.S...]
    convert_element_type x0 -> x1, other arithmetic: none -> 3.49 us  [on_device(): upstream_rows.reshape(expert_rows.shape).astype(jnp.float32)]
    dot_general x0 -> x1, matrix products: none -> 3.31 us  [on_device(): jnp.dot(slot_pick, cotangent, preferred_element_type=jnp.float32)]
    pallas_call x1, Pallas kernels: 44.2 us -> 46.7 us  [combine(): pl.pallas_call(functools.partial(combine_kernel, groups), out_shape=jax.S...]
    unnamed x87 -> x73, local copies, waits for them, and re-layouts: 13.6 us -> 14.1 us
  transfers between devices with their start and end apart: 2 -> 1, of which waited for: 0 -> 0; matrix products, arithmetic and copies ran while one was open for 7% -> 6% of each run, Pallas kernels for 19% -> 21%
where the time goes in v3:
time: 219 us; the launch traced here: 215 us
  Pallas kernels  138 us (63%)
  matrix products  33.7 us (15%)
  local copies, waits for them, and re-layouts  19.6 us (9%)
  other arithmetic  15.1 us (7%)
  starting transfers between devices  7.4 us (3%)
    pallas_call x1, Pallas kernels, combine(): pl.pallas_call(functools.partial(combine_kernel, groups), out_shape=jax.S...  46.7 us
    pallas_call x1, Pallas kernels, finish(): pl.pallas_call(functools.partial(finish_kernel, groups), out_shape=(jax.S...  41.6 us
    pallas_call x1, Pallas kernels, dispatch(): pl.pallas_call(functools.partial(dispatch_kernel, groups), out_shape=jax....  25.4 us
    unnamed x73, local copies, waits for them, and re-layouts  14.1 us
    pallas_call x1, Pallas kernels, tensor_total(): pl.pallas_call(tensor_sum_kernel, out_shape=jax.ShapeDtypeStruct((rows, w...  13.9 us
    pallas_call x2, Pallas kernels, local_call(): pl.pallas_call(kernel, out_shape=outs, in_specs=[vmem()] * len(args), out...  10.7 us
    all_to_all x1, starting transfers between devices, on_device(): lax.all_to_all(upstream_slots, 'expert', split_axis=0, concat_axis=0, til...  7.4 us
    dot_general x3, matrix products, columns_dot(): lax.dot_general(left, right, (((0,), (0,)), ((), ())), preferred_element_...  7.36 us
  transfers between devices with their start and end apart: 1, of which 0 were waited for; matrix products, arithmetic and copies ran while one was open for 6% of the time, Pallas kernels for 21%

profile of v3, /device:TPU:0, one launch (start us, length us, event | category | flops | bytes accessed | tf_op | source)
XLA Modules:
  0.0 215.3 jit_solution(12162046224005000042)
XLA Ops:
  4.3 3.3 %fusion.11 = bf16[1024,768]{1,0:T(8,128)(2,1)} fusion(bf16[512,768]{1,0:T(8,128)(2,1)} %param.24, s32[512]{0:T(512)S(1)} %get-tuple-element.95), kind=kOutput, calls=%fused_computation.33 | convolution fusion | flops 806617088 | bytes 2361344 | tf_op jit(solution)/shard_map/dot_general | solution.py:648
  7.6 7.4 %all-to-all-start = ((bf16[8,128,768]{2,1,0:T(8,128)(2,1)}), bf16[8,128,768]{2,1,0:T(8,128)(2,1)}, u32[]{:S(2)}, u32[]{:S(2)}) async-start(bf16[8,128,768]{2,1,0:T(8,128)(2,1)} %bitcast.21), calls=%async_computation | async-start | bytes 3145728 | tf_op jit(solution)/shard_map/all_to_all | solution.py:653
  15.8 1.9 fusion.39
  18.6 4.9 %shard_map.204 = (bf16[512,192]{1,0:T(8,128)(2,1)S(1)}, f32[3,512,1]{2,1,0:T(8,128)S(1)}) custom-call(bf16[3,512,192]{2,1,0:T(8,128)(2,1)S(1)} %bitcast.96, f32[3,1024]{1,0:T(4,128)S(1)} %convolution_bitcast_fusion.2.line_ref, s32[512,1]{1,0:T(8,128)S(1)} %copy.77.column_ref, s32[1,512]{1,0:T(1,128)S(1)} %bitcast.100), custom_call_target="tpu_custom_call" | custom-call | flops 1000000000 | bytes 30000000 | tf_op jit(solution)/shard_map/pallas_call | solution.py:586
  24.5 13.9 %shard_map.205 = f32[512,768]{1,0:T(8,128)S(1)} custom-call(bf16[512,768]{1,0:T(8,128)(2,1)S(1)} %convolution_convert_fusion.3.refs_0_), custom_call_target="tpu_custom_call" | custom-call | bytes 30000000 | tf_op jit(solution)/shard_map/pallas_call | solution.py:140
  40.8 1.6 convolution_convert_fusion.4
  42.4 25.4 %shard_map.206 = bf16[4,8,32,896]{3,2,1,0:T(8,128)(2,1)S(1)} custom-call(bf16[8,32,896]{2,1,0:T(8,128)(2,1)S(1)} %bitcast.98), custom_call_target="tpu_custom_call" | custom-call | bytes 50000000 | tf_op jit(solution)/shard_map/pallas_call | solution.py:240
  69.2 3.1 %fusion.18 = f32[1024,768]{1,0:T(8,128)S(1)} fusion(bf16[1024,896]{1,0:T(8,128)(2,1)} %bitcast.92, bf16[1,768,768]{2,1,0:T(8,128)(2,1)} %param.22), kind=kOutput, calls=%fused_computation.51 | convolution fusion | flops 1207959552 | bytes 5898240 | tf_op jit(solution)/shard_map/dot_general | solution.py:704
  72.4 1.7 copy-done.33
  74.1 3.1 %convolution_convert_fusion.1 = bf16[1024,768]{1,0:T(8,128)(2,1)} fusion(bf16[1,768,768]{2,1,0:T(8,128)(2,1)S(1)} %copy-done, f32[1024,768]{1,0:T(8,128)S(1)} %fusion.18), kind=kOutput, calls=%fused_computation.35 | convolution fusion | flops 1215823872 | bytes 5898240 | tf_op jit(solution)/shard_map/dot_general | solution.py:707
  77.2 3.5 %convert_bitcast_fusion = f32[4,8,32,768]{3,2,0,1:T(8,128)} fusion(bf16[8,4,32,768]{3,2,1,0:T(8,128)(2,1)} %bitcast.37), kind=kLoop, calls=%fused_computation.12 | loop fusion | flops 786432 | bytes 4718592 | tf_op jit(solution)/shard_map/convert_element_type | solution.py:700
  80.7 1.7 multiply_convert_fusion
  82.6 1.8 copy-done.34
  84.3 4.1 %fusion.3 = bf16[1024,768]{1,0:T(8,128)(2,1)S(1)} fusion(f32[1024,768]{1,0:T(8,128)S(1)} %copy-done.34, bf16[1024,768]{1,0:T(8,128)(2,1)S(1)} %bitcast.103, bf16[1,768,768]{2,1,0:T(8,128)(2,1)S(1)} %copy-done), kind=kOutput, calls=%fused_computation.7 | convolution fusion | flops 1226833920 | bytes 7471104 | tf_op jit(solution)/shard_map/dot_general | solution.py:506
  88.4 2.9 %convolution_bitcast_fusion.1 = f32[1,768,768]{2,1,0:T(8,128)} fusion(bf16[1024,768]{1,0:T(8,128)(2,1)S(1)} %fusion.3, bf16[1024,896]{1,0:T(8,128)(2,1)S(1)} %bitcast.93), kind=kOutput, calls=%fused_computation.32 | convolution fusion | flops 1207959552 | bytes 5505024 | tf_op jit(solution)/shard_map/dot_general | solution.py:512
  92.7 46.7 %shard_map.207 = bf16[2,4,8,32,768]{4,3,2,1,0:T(8,128)(2,1)S(1)} custom-call(bf16[4,8,32,768]{3,2,1,0:T(8,128)(2,1)S(1)} %bitcast.94, bf16[4,8,32,768]{3,2,1,0:T(8,128)(2,1)S(1)} %bitcast.95), custom_call_target="tpu_custom_call" | custom-call | bytes 120000000 | tf_op jit(solution)/shard_map/pallas_call | solution.py:345
  143.2 1.4 multiply_reduce_fusion
  144.7 1.5 convert_add_fusion.1
  149.6 5.8 %shard_map.208 = (bf16[3,512,192]{2,1,0:T(8,128)(2,1)S(1)}, f32[3,1024]{1,0:T(4,128)S(1)}) custom-call(bf16[3,512,192]{2,1,0:T(8,128)(2,1)S(1)} %bitcast.97, f32[3,1024]{1,0:T(4,128)S(1)} %convolution_bitcast_fusion.2.line_ref, s32[512,1]{1,0:T(8,128)S(1)} %copy.77.column_ref, s32[1,512]{1,0:T(1,128)S(1)} %bitcast.101, f32[3,512,1]{2,1,0:T(8,128)S(1)} %copy-done.8, ...), custom_call_target="tpu_custom_call" | custom-call | flops 1000000000 | bytes 30000000 | tf_op jit(solution)/shard_map/pallas_call | solution.py:586
  156.6 1.7 convolution_convert_fusion.2
  159.8 41.6 %shard_map.209 = (f32[512,768]{1,0:T(8,128)S(1)}, bf16[8,96,768]{2,1,0:T(8,128)(2,1)S(1)}, f32[16,768]{1,0:T(8,128)S(1)}) custom-call(bf16[512,768]{1,0:T(8,128)(2,1)S(1)} %bitcast_convert_fusion.x_ref, f32[512,768]{1,0:T(8,128)S(1)} %get-tuple-element.94.unit_ref, bf16[8,96,768]{2,1,0:T(8,128)(2,1)S(1)} %bitcast.90, f32[16,768]{1,0:T(8,128)S(1)} %pad.14.small_ref), custom_call_target="tpu_custom_call" | custom-call | bytes 100000000 | tf_op jit(solution)/shard_map/pallas_call | solution.py:474
  206.6 1.6 copy-done.35
  208.3 3.3 %convolution_bitcast_fusion = f32[1,768,768]{2,1,0:T(8,128)} fusion(bf16[1024,768]{1,0:T(8,128)(2,1)S(1)} %fusion.6, f32[1024,768]{1,0:T(8,128)S(1)} %copy-done.35), kind=kOutput, calls=%fused_computation.31 | convolution fusion | flops 1215037440 | bytes 7077888 | tf_op jit(solution)/shard_map/dot_general | solution.py:512
  212.9 1.6 fusion.13
  (131 shorter events, 28.7 us)
Async XLA Ops:
  0.6 73.4 %copy-start = (bf16[1,768,768]{2,1,0:T(8,128)(2,1)S(1)}, bf16[1,768,768]{2,1,0:T(8,128)(2,1)}, u32[]{:S(2)}) copy-start(bf16[1,768,768]{2,1,0:T(8,128)(2,1)} %param.23) | copy-start | bytes 3538948
  7.6 7.4 %copy-start.32 = (s32[1,4]{1,0:T(1,128)S(1)}, s32[1,4]{1,0:T(1,128)}, u32[]{:S(2)}) copy-start(s32[1,4]{1,0:T(1,128)} %param.14) | copy-start | bytes 52
  7.6 7.7 %copy-start.14 = (bf16[512,768]{1,0:T(8,128)(2,1)S(1)}, bf16[512,768]{1,0:T(8,128)(2,1)}, u32[]{:S(2)}) copy-start(bf16[512,768]{1,0:T(8,128)(2,1)} %param.13) | copy-start | bytes 2359300
  7.6 7.9 %copy-start.28 = (s32[15]{0:T(128)S(1)}, s32[15]{0:T(128)}, u32[]{:S(2)}) copy-start(s32[15]{0:T(128)} %constant.84.clone) | copy-start | bytes 184
  7.6 8.2 %copy-start.27 = (f32[768]{0:T(1024)S(1)}, f32[768]{0:T(1024)}, u32[]{:S(2)}) copy-start(f32[768]{0:T(1024)} %param.16) | copy-start | bytes 9220
  7.6 69.6 %all-to-all-start = ((bf16[8,128,768]{2,1,0:T(8,128)(2,1)}), bf16[8,128,768]{2,1,0:T(8,128)(2,1)}, u32[]{:S(2)}, u32[]{:S(2)}) async-start(bf16[8,128,768]{2,1,0:T(8,128)(2,1)} %bitcast.21), calls=%async_computation | async-start | bytes 3145728 | tf_op jit(solution)/shard_map/all_to_all | solution.py:653
  18.4 5.1 %copy-start.5 = (bf16[512,3,192]{2,0,1:T(8,128)(2,1)}, bf16[512,3,192]{2,0,1:T(8,128)(2,1)S(1)}, u32[]{:S(2)}) copy-start(bf16[512,3,192]{2,0,1:T(8,128)(2,1)S(1)} %copy.76) | copy-start | bytes 1769476
  18.6 5.0 %copy-start.21 = (bf16[192,768]{1,0:T(8,128)(2,1)S(1)}, bf16[192,768]{1,0:T(8,128)(2,1)}, u32[]{:S(2)}) copy-start(bf16[192,768]{1,0:T(8,128)(2,1)} %param.18) | copy-start | bytes 884740
  23.6 14.9 %copy-start.15 = (bf16[512,768]{1,0:T(8,128)(2,1)S(1)}, bf16[512,768]{1,0:T(8,128)(2,1)}, u32[]{:S(2)}) copy-start(bf16[512,768]{1,0:T(8,128)(2,1)} %param.13) | copy-start | bytes 2359300
  39.1 1.4 copy-start.24
  72.4 1.7 copy-start.33
  82.4 1.9 copy-start.34
  84.3 4.1 %copy-start.3 = (bf16[4,8,32,896]{3,2,1,0:T(8,128)(2,1)S(1)}, bf16[4,8,32,896]{3,2,1,0:T(8,128)(2,1)}, u32[]{:S(2)}) copy-start(bf16[4,8,32,896]{3,2,1,0:T(8,128)(2,1)} %copy-done.2) | copy-start | bytes 5505028
  88.4 2.9 %copy-start.29 = (bf16[1,768,768]{2,1,0:T(8,128)(2,1)S(1)}, bf16[1,768,768]{2,1,0:T(8,128)(2,1)}, u32[]{:S(2)}) copy-start(bf16[1,768,768]{2,1,0:T(8,128)(2,1)} %param.22) | copy-start | bytes 3538948
  91.3 1.4 copy-start.4
  141.8 1.4 copy-start.12
  146.1 1.2 copy-start.22
  149.6 5.8 %copy-start.30 = (bf16[3,768,192]{1,2,0:T(8,128)(2,1)S(1)}, bf16[3,768,192]{1,2,0:T(8,128)(2,1)}, u32[]{:S(2)}) copy-start(bf16[3,768,192]{1,2,0:T(8,128)(2,1)} %param.17) | copy-start | bytes 2654212
  156.5 2.0 copy-start.20
  203.5 2.5 %copy-start.13 = (f32[4,8,32,768]{3,2,0,1:T(8,128)S(1)}, f32[4,8,32,768]{3,2,0,1:T(8,128)}, u32[]{:S(2)}) copy-start(f32[4,8,32,768]{3,2,0,1:T(8,128)} %convert_bitcast_fusion) | copy-start | bytes 9437188
  206.4 1.9 copy-start.35
  208.3 3.3 %copy-start.17 = (bf16[512,768]{1,0:T(8,128)(2,1)S(1)}, bf16[512,768]{1,0:T(8,128)(2,1)}, u32[]{:S(2)}) copy-start(bf16[512,768]{1,0:T(8,128)(2,1)} %param.13) | copy-start | bytes 2359300
  211.5 1.4 copy-start.10
  211.8 3.4 %copy-start.1 = (bf16[1,768,768]{2,1,0:T(8,128)(2,1)S(1)}, bf16[1,768,768]{2,1,0:T(8,128)(2,1)}, u32[]{:S(2)}) copy-start(bf16[1,768,768]{2,1,0:T(8,128)(2,1)} %param.23) | copy-start | bytes 3538948
  (13 other events, 13.3 us)

commit v4 on v3

--- a/solution.py
+++ b/solution.py
@@ -313,12 +313,15 @@
 
     begin, forward = share_over_tensor(places, pieces, sems[6:])
     shared = []
+    onward = []
     for place in range(2 * groups):
         if place % groups:
             outgoing[place].wait_recv()
         shared.append(begin(place))
-    onward = []
-    for place in range(2 * groups):
+        if place >= groups:
+            shared[place - groups][0].wait_recv()
+            onward.append(forward(place - groups))
+    for place in range(groups, 2 * groups):
         shared[place][0].wait_recv()
         onward.append(forward(place))
     for copy in gather + crossing:

time: 219 us -> 219 us (level)
  no operation moved by 1% of the time
where the time goes in v4:
time: 219 us; the launch traced here: 215 us
  Pallas kernels  138 us (63%)
  matrix products  33.7 us (15%)
  local copies, waits for them, and re-layouts  19.6 us (9%)
  other arithmetic  15.1 us (7%)
  starting transfers between devices  7.4 us (3%)
    pallas_call x1, Pallas kernels, combine(): pl.pallas_call(functools.partial(combine_kernel, groups), out_shape=jax.S...  46.7 us
    pallas_call x1, Pallas kernels, finish(): pl.pallas_call(functools.partial(finish_kernel, groups), out_shape=(jax.S...  41.6 us
    pallas_call x1, Pallas kernels, dispatch(): pl.pallas_call(functools.partial(dispatch_kernel, groups), out_shape=jax....  25.4 us
    unnamed x73, local copies, waits for them, and re-layouts  14.1 us
    pallas_call x1, Pallas kernels, tensor_total(): pl.pallas_call(tensor_sum_kernel, out_shape=jax.ShapeDtypeStruct((rows, w...  13.9 us
    pallas_call x2, Pallas kernels, local_call(): pl.pallas_call(kernel, out_shape=outs, in_specs=[vmem()] * len(args), out...  10.7 us
    all_to_all x1, starting transfers between devices, on_device(): lax.all_to_all(upstream_slots, 'expert', split_axis=0, concat_axis=0, til...  7.4 us
    dot_general x3, matrix products, columns_dot(): lax.dot_general(left, right, (((0,), (0,)), ((), ())), preferred_element_...  7.36 us
  transfers between devices with their start and end apart: 1, of which 0 were waited for; matrix products, arithmetic and copies ran while one was open for 6% of the time, Pallas kernels for 21%

profile of v4, /device:TPU:0, one launch (start us, length us, event | category | flops | bytes accessed | tf_op | source)
XLA Modules:
  0.0 215.3 jit_solution(3404873519461126550)
XLA Ops:
  4.3 3.3 %fusion.11 = bf16[1024,768]{1,0:T(8,128)(2,1)} fusion(bf16[512,768]{1,0:T(8,128)(2,1)} %param.24, s32[512]{0:T(512)S(1)} %get-tuple-element.95), kind=kOutput, calls=%fused_computation.33 | convolution fusion | flops 806617088 | bytes 2361344 | tf_op jit(solution)/shard_map/dot_general | solution.py:651
  7.6 7.4 %all-to-all-start = ((bf16[8,128,768]{2,1,0:T(8,128)(2,1)}), bf16[8,128,768]{2,1,0:T(8,128)(2,1)}, u32[]{:S(2)}, u32[]{:S(2)}) async-start(bf16[8,128,768]{2,1,0:T(8,128)(2,1)} %bitcast.21), calls=%async_computation | async-start | bytes 3145728 | tf_op jit(solution)/shard_map/all_to_all | solution.py:656
  15.8 1.9 fusion.39
  18.6 4.9 %shard_map.204 = (bf16[512,192]{1,0:T(8,128)(2,1)S(1)}, f32[3,512,1]{2,1,0:T(8,128)S(1)}) custom-call(bf16[3,512,192]{2,1,0:T(8,128)(2,1)S(1)} %bitcast.96, f32[3,1024]{1,0:T(4,128)S(1)} %convolution_bitcast_fusion.2.line_ref, s32[512,1]{1,0:T(8,128)S(1)} %copy.77.column_ref, s32[1,512]{1,0:T(1,128)S(1)} %bitcast.100), custom_call_target="tpu_custom_call" | custom-call | flops 1000000000 | bytes 30000000 | tf_op jit(solution)/shard_map/pallas_call | solution.py:589
  24.5 13.9 %shard_map.205 = f32[512,768]{1,0:T(8,128)S(1)} custom-call(bf16[512,768]{1,0:T(8,128)(2,1)S(1)} %convolution_convert_fusion.3.refs_0_), custom_call_target="tpu_custom_call" | custom-call | bytes 30000000 | tf_op jit(solution)/shard_map/pallas_call | solution.py:140
  40.8 1.6 convolution_convert_fusion.4
  42.4 25.4 %shard_map.206 = bf16[4,8,32,896]{3,2,1,0:T(8,128)(2,1)S(1)} custom-call(bf16[8,32,896]{2,1,0:T(8,128)(2,1)S(1)} %bitcast.98), custom_call_target="tpu_custom_call" | custom-call | bytes 50000000 | tf_op jit(solution)/shard_map/pallas_call | solution.py:240
  69.2 3.1 %fusion.18 = f32[1024,768]{1,0:T(8,128)S(1)} fusion(bf16[1024,896]{1,0:T(8,128)(2,1)} %bitcast.92, bf16[1,768,768]{2,1,0:T(8,128)(2,1)} %param.22), kind=kOutput, calls=%fused_computation.51 | convolution fusion | flops 1207959552 | bytes 5898240 | tf_op jit(solution)/shard_map/dot_general | solution.py:707
  72.4 1.7 copy-done.33
  74.1 3.1 %convolution_convert_fusion.1 = bf16[1024,768]{1,0:T(8,128)(2,1)} fusion(bf16[1,768,768]{2,1,0:T(8,128)(2,1)S(1)} %copy-done, f32[1024,768]{1,0:T(8,128)S(1)} %fusion.18), kind=kOutput, calls=%fused_computation.35 | convolution fusion | flops 1215823872 | bytes 5898240 | tf_op jit(solution)/shard_map/dot_general | solution.py:710
  77.2 3.5 %convert_bitcast_fusion = f32[4,8,32,768]{3,2,0,1:T(8,128)} fusion(bf16[8,4,32,768]{3,2,1,0:T(8,128)(2,1)} %bitcast.37), kind=kLoop, calls=%fused_computation.12 | loop fusion | flops 786432 | bytes 4718592 | tf_op jit(solution)/shard_map/convert_element_type | solution.py:703
  80.7 1.7 multiply_convert_fusion
  82.6 1.8 copy-done.34
  84.3 4.1 %fusion.3 = bf16[1024,768]{1,0:T(8,128)(2,1)S(1)} fusion(f32[1024,768]{1,0:T(8,128)S(1)} %copy-done.34, bf16[1024,768]{1,0:T(8,128)(2,1)S(1)} %bitcast.103, bf16[1,768,768]{2,1,0:T(8,128)(2,1)S(1)} %copy-done), kind=kOutput, calls=%fused_computation.7 | convolution fusion | flops 1226833920 | bytes 7471104 | tf_op jit(solution)/shard_map/dot_general | solution.py:509
  88.4 2.9 %convolution_bitcast_fusion.1 = f32[1,768,768]{2,1,0:T(8,128)} fusion(bf16[1024,768]{1,0:T(8,128)(2,1)S(1)} %fusion.3, bf16[1024,896]{1,0:T(8,128)(2,1)S(1)} %bitcast.93), kind=kOutput, calls=%fused_computation.32 | convolution fusion | flops 1207959552 | bytes 5505024 | tf_op jit(solution)/shard_map/dot_general | solution.py:515
  92.7 46.7 %shard_map.207 = bf16[2,4,8,32,768]{4,3,2,1,0:T(8,128)(2,1)S(1)} custom-call(bf16[4,8,32,768]{3,2,1,0:T(8,128)(2,1)S(1)} %bitcast.94, bf16[4,8,32,768]{3,2,1,0:T(8,128)(2,1)S(1)} %bitcast.95), custom_call_target="tpu_custom_call" | custom-call | bytes 120000000 | tf_op jit(solution)/shard_map/pallas_call | solution.py:348
  143.2 1.4 multiply_reduce_fusion
  144.7 1.5 convert_add_fusion.1
  149.6 5.8 %shard_map.208 = (bf16[3,512,192]{2,1,0:T(8,128)(2,1)S(1)}, f32[3,1024]{1,0:T(4,128)S(1)}) custom-call(bf16[3,512,192]{2,1,0:T(8,128)(2,1)S(1)} %bitcast.97, f32[3,1024]{1,0:T(4,128)S(1)} %convolution_bitcast_fusion.2.line_ref, s32[512,1]{1,0:T(8,128)S(1)} %copy.77.column_ref, s32[1,512]{1,0:T(1,128)S(1)} %bitcast.101, f32[3,512,1]{2,1,0:T(8,128)S(1)} %copy-done.8, ...), custom_call_target="tpu_custom_call" | custom-call | flops 1000000000 | bytes 30000000 | tf_op jit(solution)/shard_map/pallas_call | solution.py:589
  156.6 1.7 convolution_convert_fusion.2
  159.8 41.6 %shard_map.209 = (f32[512,768]{1,0:T(8,128)S(1)}, bf16[8,96,768]{2,1,0:T(8,128)(2,1)S(1)}, f32[16,768]{1,0:T(8,128)S(1)}) custom-call(bf16[512,768]{1,0:T(8,128)(2,1)S(1)} %bitcast_convert_fusion.x_ref, f32[512,768]{1,0:T(8,128)S(1)} %get-tuple-element.94.unit_ref, bf16[8,96,768]{2,1,0:T(8,128)(2,1)S(1)} %bitcast.90, f32[16,768]{1,0:T(8,128)S(1)} %pad.14.small_ref), custom_call_target="tpu_custom_call" | custom-call | bytes 100000000 | tf_op jit(solution)/shard_map/pallas_call | solution.py:477
  206.6 1.6 copy-done.35
  208.3 3.3 %convolution_bitcast_fusion = f32[1,768,768]{2,1,0:T(8,128)} fusion(bf16[1024,768]{1,0:T(8,128)(2,1)S(1)} %fusion.6, f32[1024,768]{1,0:T(8,128)S(1)} %copy-done.35), kind=kOutput, calls=%fused_computation.31 | convolution fusion | flops 1215037440 | bytes 7077888 | tf_op jit(solution)/shard_map/dot_general | solution.py:515
  212.9 1.6 fusion.13
  (131 shorter events, 28.7 us)
Async XLA Ops:
  0.6 73.4 %copy-start = (bf16[1,768,768]{2,1,0:T(8,128)(2,1)S(1)}, bf16[1,768,768]{2,1,0:T(8,128)(2,1)}, u32[]{:S(2)}) copy-start(bf16[1,768,768]{2,1,0:T(8,128)(2,1)} %param.23) | copy-start | bytes 3538948
  7.6 7.4 %copy-start.32 = (s32[1,4]{1,0:T(1,128)S(1)}, s32[1,4]{1,0:T(1,128)}, u32[]{:S(2)}) copy-start(s32[1,4]{1,0:T(1,128)} %param.14) | copy-start | bytes 52
  7.6 7.7 %copy-start.14 = (bf16[512,768]{1,0:T(8,128)(2,1)S(1)}, bf16[512,768]{1,0:T(8,128)(2,1)}, u32[]{:S(2)}) copy-start(bf16[512,768]{1,0:T(8,128)(2,1)} %param.13) | copy-start | bytes 2359300
  7.6 7.9 %copy-start.28 = (s32[15]{0:T(128)S(1)}, s32[15]{0:T(128)}, u32[]{:S(2)}) copy-start(s32[15]{0:T(128)} %constant.84.clone) | copy-start | bytes 184
  7.6 8.2 %copy-start.27 = (f32[768]{0:T(1024)S(1)}, f32[768]{0:T(1024)}, u32[]{:S(2)}) copy-start(f32[768]{0:T(1024)} %param.16) | copy-start | bytes 9220
  7.6 69.6 %all-to-all-start = ((bf16[8,128,768]{2,1,0:T(8,128)(2,1)}), bf16[8,128,768]{2,1,0:T(8,128)(2,1)}, u32[]{:S(2)}, u32[]{:S(2)}) async-start(bf16[8,128,768]{2,1,0:T(8,128)(2,1)} %bitcast.21), calls=%async_computation | async-start | bytes 3145728 | tf_op jit(solution)/shard_map/all_to_all | solution.py:656
  18.4 5.1 %copy-start.5 = (bf16[512,3,192]{2,0,1:T(8,128)(2,1)}, bf16[512,3,192]{2,0,1:T(8,128)(2,1)S(1)}, u32[]{:S(2)}) copy-start(bf16[512,3,192]{2,0,1:T(8,128)(2,1)S(1)} %copy.76) | copy-start | bytes 1769476
  18.6 5.0 %copy-start.21 = (bf16[192,768]{1,0:T(8,128)(2,1)S(1)}, bf16[192,768]{1,0:T(8,128)(2,1)}, u32[]{:S(2)}) copy-start(bf16[192,768]{1,0:T(8,128)(2,1)} %param.18) | copy-start | bytes 884740
  23.6 14.9 %copy-start.15 = (bf16[512,768]{1,0:T(8,128)(2,1)S(1)}, bf16[512,768]{1,0:T(8,128)(2,1)}, u32[]{:S(2)}) copy-start(bf16[512,768]{1,0:T(8,128)(2,1)} %param.13) | copy-start | bytes 2359300
  39.1 1.4 copy-start.24
  72.4 1.7 copy-start.33
  82.4 1.9 copy-start.34
  84.3 4.1 %copy-start.3 = (bf16[4,8,32,896]{3,2,1,0:T(8,128)(2,1)S(1)}, bf16[4,8,32,896]{3,2,1,0:T(8,128)(2,1)}, u32[]{:S(2)}) copy-start(bf16[4,8,32,896]{3,2,1,0:T(8,128)(2,1)} %copy-done.2) | copy-start | bytes 5505028
  88.4 2.9 %copy-start.29 = (bf16[1,768,768]{2,1,0:T(8,128)(2,1)S(1)}, bf16[1,768,768]{2,1,0:T(8,128)(2,1)}, u32[]{:S(2)}) copy-start(bf16[1,768,768]{2,1,0:T(8,128)(2,1)} %param.22) | copy-start | bytes 3538948
  91.3 1.4 copy-start.4
  141.8 1.4 copy-start.12
  146.1 1.2 copy-start.22
  149.6 5.8 %copy-start.30 = (bf16[3,768,192]{1,2,0:T(8,128)(2,1)S(1)}, bf16[3,768,192]{1,2,0:T(8,128)(2,1)}, u32[]{:S(2)}) copy-start(bf16[3,768,192]{1,2,0:T(8,128)(2,1)} %param.17) | copy-start | bytes 2654212
  156.5 2.0 copy-start.20
  203.5 2.5 %copy-start.13 = (f32[4,8,32,768]{3,2,0,1:T(8,128)S(1)}, f32[4,8,32,768]{3,2,0,1:T(8,128)}, u32[]{:S(2)}) copy-start(f32[4,8,32,768]{3,2,0,1:T(8,128)} %convert_bitcast_fusion) | copy-start | bytes 9437188
  206.4 1.9 copy-start.35
  208.3 3.3 %copy-start.17 = (bf16[512,768]{1,0:T(8,128)(2,1)S(1)}, bf16[512,768]{1,0:T(8,128)(2,1)}, u32[]{:S(2)}) copy-start(bf16[512,768]{1,0:T(8,128)(2,1)} %param.13) | copy-start | bytes 2359300
  211.5 1.4 copy-start.10
  211.8 3.4 %copy-start.1 = (bf16[1,768,768]{2,1,0:T(8,128)(2,1)S(1)}, bf16[1,768,768]{2,1,0:T(8,128)(2,1)}, u32[]{:S(2)}) copy-start(bf16[1,768,768]{2,1,0:T(8,128)(2,1)} %param.23) | copy-start | bytes 3538948
  (13 other events, 13.3 us)
